TPU v7x, 512 devices: a whole 4x4x16 slice. The times are simulated.
512 devices in a mesh: fsdp: 32 (over y, x, core), expert: 16 (over z).
Axes of the slice: x: 4, y: 4, z: 16, core: 2. Of those that a mesh axis runs over, the one named last changes fastest.
Arguments:
- tokens: bfloat16 [65536, 2048], P(('fsdp', 'expert')), may hold values from -6 to 6
- cotangent: bfloat16 [65536, 2048], P(('fsdp', 'expert')), may hold values from -6 to 6
- routes: int32 [65536, 8], P(('fsdp', 'expert')), may hold values from 0 to 127, all different within a row
- route_weights: float32 [65536, 8], P(('fsdp', 'expert')), may hold values from 0.05 to 0.8
- gate_up_weight: bfloat16 [16, 2048, 1536], P('expert', 'fsdp'), may hold values from -0.125 to 0.125
- down_weight: bfloat16 [16, 2048, 768], P('expert', 'fsdp'), may hold values from -0.21875 to 0.21875
Outputs:
- mixed: bfloat16 [65536, 2048], P(('fsdp', 'expert'))
- grad_tokens: bfloat16 [65536, 2048], P(('fsdp', 'expert'))
- grad_gates: float32 [65536, 8], P(('fsdp', 'expert'))
Inputs may be any that keep to these rules, and one draw needn't show every extreme that they name: `routes`: each row names 8 different experts.
All inputs are finite; a program needn't handle non-finite values.
Results may differ from a plain program's by a relative error of at most 0.0062.
Values may be sent and summed in bfloat16 or wider, within the bound.
A program may use at most 64 MiB of HBM per device.

v0:
```python
import jax
import jax.numpy as jnp
from jax import lax
from jax.sharding import PartitionSpec as P

contract_last = (((1,), (1,)), ((), ()))


def route_slots(routes, groups, capacity):
    experts = jnp.arange(groups, dtype=jnp.int32)
    matches = (routes[:, :, None] == experts).astype(jnp.int32)
    counts = jnp.sum(matches, axis=1, dtype=jnp.int32)
    earlier = jnp.cumsum(counts, axis=0, dtype=jnp.int32) - counts
    slot_ids = jnp.sum(matches * earlier[:, None, :], axis=2, dtype=jnp.int32)
    is_kept = (routes < groups) & (slot_ids < capacity)
    return jnp.where(is_kept, routes * capacity + slot_ids, groups * capacity)


def forward_units(stacked, gate_up_mat, down_mat):
    gate_up = jnp.dot(stacked, gate_up_mat, preferred_element_type=jnp.float32)
    middle = gate_up.shape[1] // 2
    gate_part = gate_up[:, :middle]
    up_part = gate_up[:, middle:]
    hidden = (jax.nn.silu(gate_part) * up_part).astype(jnp.bfloat16)
    partial_out = lax.dot_general(
        hidden, down_mat, contract_last, preferred_element_type=jnp.float32
    )
    return (partial_out, (gate_part, up_part))


def backward_units(grad_rows, stored, gate_up_mat, down_mat):
    gate_part, up_part = stored
    grad_hidden = jnp.dot(grad_rows, down_mat, preferred_element_type=jnp.float32)
    sigmoid_gate = jax.nn.sigmoid(gate_part)
    grad_gate = grad_hidden * up_part * sigmoid_gate * (1.0 + gate_part * (1.0 - sigmoid_gate))
    grad_up = grad_hidden * gate_part * sigmoid_gate
    grad_gate_up = jnp.concatenate([grad_gate, grad_up], 1).astype(jnp.bfloat16)
    return lax.dot_general(
        grad_gate_up, gate_up_mat, contract_last, preferred_element_type=jnp.float32
    )


def whole_forward(expert_rows, weights):
    partial_out, stored = forward_units(expert_rows, weights[0], weights[1])
    return (partial_out.astype(jnp.bfloat16), stored)


def whole_backward(grad_rows, stored, weights):
    return backward_units(grad_rows, stored, weights[0], weights[1]).astype(jnp.bfloat16)


def on_device(tokens, cotangent, routes, route_weights, gate_up_weight, down_weight):
    groups = lax.axis_size("expert")
    tok_rows, width = tokens.shape
    capacity = 3 * tok_rows // 32
    buffer_rows = groups * capacity
    targets = route_slots(routes, groups, capacity)
    flat_targets = targets.reshape(-1)
    token_ids = jnp.broadcast_to(
        jnp.arange(tok_rows, dtype=jnp.int32)[:, None], targets.shape
    ).reshape(-1)
    owners = (
        jnp.full((buffer_rows + 1,), tok_rows, jnp.int32)
        .at[flat_targets]
        .set(token_ids)[:buffer_rows]
    )
    slot_weights = (
        jnp.zeros((buffer_rows + 1,), jnp.float32)
        .at[flat_targets]
        .set(route_weights.reshape(-1))[:buffer_rows]
    )
    blank_row = jnp.zeros((1, width), jnp.bfloat16)
    padded_tokens = jnp.concatenate([tokens, blank_row], 0)
    padded_cot = jnp.concatenate([cotangent, blank_row], 0)
    send_tokens = padded_tokens[owners].reshape(groups, capacity, width)
    send_grads = (
        (slot_weights[:, None] * padded_cot[owners].astype(jnp.float32))
        .astype(jnp.bfloat16)
        .reshape(groups, capacity, width)
    )
    gathered = (
        lax.all_gather(gate_up_weight, "fsdp", axis=1, tiled=True),
        lax.all_gather(down_weight, "fsdp", axis=1, tiled=True),
    )
    weights = (gathered[0][0], gathered[1][0])
    arrived = lax.all_to_all(send_tokens, "expert", split_axis=0, concat_axis=0, tiled=True)
    expert_out, stored = whole_forward(arrived.reshape(-1, width), weights)
    out_back = lax.all_to_all(
        expert_out.reshape(groups, capacity, width),
        "expert",
        split_axis=0,
        concat_axis=0,
        tiled=True,
    )
    arrived_grads = lax.all_to_all(send_grads, "expert", split_axis=0, concat_axis=0, tiled=True)
    expert_grad = whole_backward(arrived_grads.reshape(-1, width), stored, weights)
    grad_back = lax.all_to_all(
        expert_grad.reshape(groups, capacity, width),
        "expert",
        split_axis=0,
        concat_axis=0,
        tiled=True,
    )
    padded_out = jnp.concatenate([out_back.reshape(-1, width), blank_row], 0)
    padded_grad = jnp.concatenate([grad_back.reshape(-1, width), blank_row], 0)
    returned = padded_out[targets].astype(jnp.float32)
    returned_grads = padded_grad[targets].astype(jnp.float32)
    mixed = jnp.sum(route_weights[:, :, None] * returned, axis=1)
    grad_sum = jnp.sum(returned_grads, axis=1)
    gate_columns = jnp.sum(returned * cotangent.astype(jnp.float32)[:, None, :], axis=2)
    return (mixed.astype(jnp.bfloat16), grad_sum.astype(jnp.bfloat16), gate_columns)


def solution(mesh):
    return jax.shard_map(
        on_device,
        mesh=mesh,
        in_specs=(
            P(("fsdp", "expert"), None),
            P(("fsdp", "expert"), None),
            P(("fsdp", "expert"), None),
            P(("fsdp", "expert"), None),
            P("expert", "fsdp", None),
            P("expert", "fsdp", None),
        ),
        out_specs=(
            P(("fsdp", "expert"), None),
            P(("fsdp", "expert"), None),
            P(("fsdp", "expert"), None),
        ),
        check_vma=False,
    )
```

profile of v0, /device:TPU:1, one launch (start us, length us, event | category | flops | bytes accessed | tf_op | source)
XLA Modules:
  0.0 290.8 jit_solution(18069511277634468207)
XLA Ops:
  7.2 0.0 all-gather.3.cloned.1.call-start
  7.2 0.7 all-gather.3.cloned.1.call-update
  7.9 0.7 convert_reduce_fusion
  8.6 0.1 copy.23
  8.7 0.2 reduce_window_sum.11
  8.9 0.1 copy.25
  8.9 0.7 select_reduce_fusion
  9.7 0.7 compare_select_fusion.1
  10.4 0.1 copy.26
  10.5 0.1 reshape.86
  10.6 0.1 reshape.133
  10.7 1.1 concatenate.18
  11.8 4.3 %scatter_custom_fusion = s32[193]{0:T(256)S(1)} fusion(s32[1024]{0:T(1024)S(1)} %bitcast.26, s32[1024]{0:T(1024)S(1)} %reshape.133, s32[]{:T(128)} %constant.11.clone.1), kind=kCustom, calls=%fused_computation.41 | custom fusion | bytes 776 | tf_op jit(solution)/shard_map/scatter | solution.py:65
  16.1 0.0 copy-start.3
  16.1 1.1 gather_fusion.2
  17.3 0.0 copy-start.2
  17.3 0.1 reshape.96
  17.4 0.0 copy-done.3
  17.5 0.1 copy.22
  17.6 0.1 reshape.141
  17.6 4.3 %scatter_custom_fusion.1 = f32[193]{0:T(256)S(1)} fusion(s32[1024]{0:T(1024)S(1)} %bitcast.27, f32[1024]{0:T(1024)S(1)} %reshape.141, f32[]{:T(128)} %constant.7.clone.1), kind=kCustom, calls=%fused_computation.39 | custom fusion | bytes 776 | tf_op jit(solution)/shard_map/scatter | solution.py:70
  22.0 0.1 mul.70
  22.0 1.2 multiply_convert_fusion
  23.2 15.7 %all-to-all-start.2 = ((bf16[16,12,2048]{2,1,0:T(8,128)(2,1)}), bf16[16,12,2048]{2,1,0:T(8,128)(2,1)S(1)}, u32[]{:S(2)}, u32[]{:S(2)}) async-start(bf16[16,12,2048]{2,1,0:T(8,128)(2,1)} %multiply_convert_fusion), calls=%async_computation.2 | async-start | bytes 2097152 | tf_op jit(solution)/shard_map/all_to_all | solution.py:95
  39.0 0.0 all-gather.5.cloned.1.call-start
  39.0 0.7 all-gather.5.cloned.1.call-update
  39.7 0.0 copy-done.2
  39.8 1.1 gather_fusion
  40.9 1.1 reshape.88
  42.1 41.7 %all-to-all-done.2 = bf16[16,12,2048]{2,1,0:T(8,128)(2,1)S(1)} async-done(((bf16[16,12,2048]{2,1,0:T(8,128)(2,1)}), bf16[16,12,2048]{2,1,0:T(8,128)(2,1)S(1)}, u32[]{:S(2)}, u32[]{:S(2)}) %all-to-all-start.2) | async-done | bytes 786464 | tf_op jit(solution)/shard_map/all_to_all | solution.py:95
  83.8 13.2 %all-to-all-start = ((bf16[16,12,2048]{2,1,0:T(8,128)(2,1)}), bf16[16,12,2048]{2,1,0:T(8,128)(2,1)S(1)}, u32[]{:S(2)}, u32[]{:S(2)}) async-start(bf16[16,12,2048]{2,1,0:T(8,128)(2,1)} %reshape.88), calls=%async_computation | async-start | bytes 2097152 | tf_op jit(solution)/shard_map/all_to_all | solution.py:86
  97.0 0.2 reshape.93
  97.2 45.1 %all-to-all-done = bf16[16,12,2048]{2,1,0:T(8,128)(2,1)S(1)} async-done(((bf16[16,12,2048]{2,1,0:T(8,128)(2,1)}), bf16[16,12,2048]{2,1,0:T(8,128)(2,1)S(1)}, u32[]{:S(2)}, u32[]{:S(2)}) %all-to-all-start) | async-done | bytes 786464 | tf_op jit(solution)/shard_map/all_to_all | solution.py:86
  142.2 0.2 reshape.89
  142.4 0.0 all-gather.3.cloned.1.call-done
  142.4 5.2 %fusion.4 = f32[192,1536]{1,0:T(8,128)} fusion(bf16[192,2048]{1,0:T(8,128)(2,1)S(1)} %reshape.89, bf16[1,2048,1536]{2,1,0:T(8,128)(2,1)} %all-gather.3.cloned.1.call-done), kind=kOutput, calls=%fused_computation.12 | convolution fusion | flops 1207959552 | bytes 8257536 | tf_op jit(solution)/shard_map/dot_general | solution.py:20
  147.7 0.0 all-gather.5.cloned.1.call-done
  147.7 0.0 copy-start.4
  147.7 3.2 %multiply_convert_fusion.2 = (bf16[192,768]{1,0:T(8,128)(2,1)S(1)}, bf16[192,768]{1,0:T(8,128)(2,1)S(1)}) fusion(f32[192,1536]{1,0:T(8,128)} %fusion.4, bf16[192,2048]{1,0:T(8,128)(2,1)S(1)} %reshape.93, bf16[1,2048,768]{2,1,0:T(8,128)(2,1)} %all-gather.5.cloned.1.call-done), kind=kOutput, calls=%fused_computation.26 | convolution fusion | flops 605896704 | bytes 5701632 | tf_op jit(solution)/shard_map/dot_general | solution.py:33
  150.9 0.8 copy-done.4
  151.7 2.2 fusion.13
  153.9 1.2 reshape.94
  155.1 12.8 %all-to-all-start.3 = ((bf16[16,12,2048]{2,1,0:T(8,128)(2,1)}), bf16[16,12,2048]{2,1,0:T(8,128)(2,1)S(1)}, u32[]{:S(2)}, u32[]{:S(2)}) async-start(bf16[16,12,2048]{2,1,0:T(8,128)(2,1)} %reshape.94), calls=%async_computation.3 | async-start | bytes 2097152 | tf_op jit(solution)/shard_map/all_to_all | solution.py:97
  167.9 0.0 copy-start.1
  167.9 3.5 %fusion.10 = bf16[192,2048]{1,0:T(8,128)(2,1)S(1)} fusion(bf16[1,2048,768]{2,1,0:T(8,128)(2,1)} %all-gather.5.cloned.1.call-done, f32[192,1536]{1,0:T(8,128)} %fusion.4), kind=kOutput, calls=%fused_computation.19 | convolution fusion | flops 605257728 | bytes 5111808 | tf_op jit(solution)/shard_map/dot_general | solution.py:25
  171.4 1.1 reshape.90
  172.6 40.6 %all-to-all-done.3 = bf16[16,12,2048]{2,1,0:T(8,128)(2,1)S(1)} async-done(((bf16[16,12,2048]{2,1,0:T(8,128)(2,1)}), bf16[16,12,2048]{2,1,0:T(8,128)(2,1)S(1)}, u32[]{:S(2)}, u32[]{:S(2)}) %all-to-all-start.3) | async-done | bytes 786464 | tf_op jit(solution)/shard_map/all_to_all | solution.py:97
  213.1 12.8 %all-to-all-start.1 = ((bf16[16,12,2048]{2,1,0:T(8,128)(2,1)}), bf16[16,12,2048]{2,1,0:T(8,128)(2,1)S(1)}, u32[]{:S(2)}, u32[]{:S(2)}) async-start(bf16[16,12,2048]{2,1,0:T(8,128)(2,1)} %reshape.90), calls=%async_computation.1 | async-start | bytes 2097152 | tf_op jit(solution)/shard_map/all_to_all | solution.py:88
  226.0 0.0 copy-done.1
  226.0 1.1 convert_element_type.44
  227.1 0.1 copy.27
  227.2 0.1 reshape.107
  227.3 0.2 reshape.95
  227.5 0.1 concatenate.20
  227.6 6.0 %gather_fusion.3 = bf16[1024,2048]{1,0:T(8,128)(2,1)} fusion(bf16[193,2048]{1,0:T(8,128)(2,1)S(1)} %concatenate.20, s32[1024]{0:T(1024)S(1)} %broadcast_clamp_fusion), kind=kCustom, calls=%fused_computation.3 | custom fusion | bytes 8392704 | tf_op jit(solution)/shard_map/gather | solution.py:107
  233.6 5.9 %bitcast_reduce_fusion = bf16[128,2048]{1,0:T(8,128)(2,1)} fusion(bf16[1024,2048]{1,0:T(8,128)(2,1)} %gather_fusion.3), kind=kLoop, calls=%fused_computation.14 | loop fusion | flops 1835008 | bytes 4718592 | tf_op jit(solution)/shard_map/reduce_sum | solution.py:109
  239.4 31.7 %all-to-all-done.1 = bf16[16,12,2048]{2,1,0:T(8,128)(2,1)S(1)} async-done(((bf16[16,12,2048]{2,1,0:T(8,128)(2,1)}), bf16[16,12,2048]{2,1,0:T(8,128)(2,1)S(1)}, u32[]{:S(2)}, u32[]{:S(2)}) %all-to-all-start.1) | async-done | bytes 786464 | tf_op jit(solution)/shard_map/all_to_all | solution.py:88
  271.2 0.2 reshape.91
  271.4 0.1 concatenate.17
  271.5 0.0 copy-start
  271.5 6.0 %gather_fusion.1 = bf16[1024,2048]{1,0:T(8,128)(2,1)} fusion(bf16[193,2048]{1,0:T(8,128)(2,1)S(1)} %concatenate.17, s32[1024]{0:T(1024)S(1)} %broadcast_clamp_fusion), kind=kCustom, calls=%fused_computation.1 | custom fusion | bytes 8392704 | tf_op jit(solution)/shard_map/gather | solution.py:106
  277.5 0.0 copy-done
  277.5 5.9 %fusion.1 = (f32[128,8]{1,0:T(8,128)S(1)}, bf16[128,2048]{1,0:T(8,128)(2,1)}) fusion(bf16[1024,2048]{1,0:T(8,128)(2,1)} %gather_fusion.1, f32[128,2048]{1,0:T(8,128)S(1)} %copy-done, f32[128,8]{1,0:T(8,128)S(1)} %copy.22), kind=kLoop, calls=%fused_computation.9 | loop fusion | flops 10222592 | bytes 5775360 | tf_op jit(solution)/shard_map/reduce_sum | solution.py:110
  283.3 0.7 copy.29
  (7 shorter events, 0.1 us)
Async XLA Ops:
  7.2 135.3 %all-gather.3.cloned.1.call-start = ((), (), s32[]{:S(2)}) async-start(), calls=%async_computation.4 | async-start | bytes 6488064 | tf_op jit(solution)/shard_map/all_gather | solution.py:82
  16.1 1.3 copy-start.3
  17.3 22.4 %copy-start.2 = (bf16[128,2048]{1,0:T(8,128)(2,1)S(1)}, bf16[128,2048]{1,0:T(8,128)(2,1)}, u32[]{:S(2)}) copy-start(bf16[128,2048]{1,0:T(8,128)(2,1)} %param.6) | copy-start | bytes 1572868
  23.2 60.6 %all-to-all-start.2 = ((bf16[16,12,2048]{2,1,0:T(8,128)(2,1)}), bf16[16,12,2048]{2,1,0:T(8,128)(2,1)S(1)}, u32[]{:S(2)}, u32[]{:S(2)}) async-start(bf16[16,12,2048]{2,1,0:T(8,128)(2,1)} %multiply_convert_fusion), calls=%async_computation.2 | async-start | bytes 2097152 | tf_op jit(solution)/shard_map/all_to_all | solution.py:95
  39.0 108.7 %all-gather.5.cloned.1.call-start = ((), (), s32[]{:S(2)}) async-start(), calls=%async_computation.5 | async-start | bytes 3244032 | tf_op jit(solution)/shard_map/all_gather | solution.py:83
  83.8 58.4 %all-to-all-start = ((bf16[16,12,2048]{2,1,0:T(8,128)(2,1)}), bf16[16,12,2048]{2,1,0:T(8,128)(2,1)S(1)}, u32[]{:S(2)}, u32[]{:S(2)}) async-start(bf16[16,12,2048]{2,1,0:T(8,128)(2,1)} %reshape.88), calls=%async_computation | async-start | bytes 2097152 | tf_op jit(solution)/shard_map/all_to_all | solution.py:86
  147.7 4.1 %copy-start.4 = (bf16[1,2048,1536]{2,1,0:T(8,128)(2,1)S(1)}, bf16[1,2048,1536]{2,1,0:T(8,128)(2,1)}, u32[]{:S(2)}) copy-start(bf16[1,2048,1536]{2,1,0:T(8,128)(2,1)} %all-gather.3.cloned.1.call-done) | copy-start | bytes 18874372
  155.1 58.0 %all-to-all-start.3 = ((bf16[16,12,2048]{2,1,0:T(8,128)(2,1)}), bf16[16,12,2048]{2,1,0:T(8,128)(2,1)S(1)}, u32[]{:S(2)}, u32[]{:S(2)}) async-start(bf16[16,12,2048]{2,1,0:T(8,128)(2,1)} %reshape.94), calls=%async_computation.3 | async-start | bytes 2097152 | tf_op jit(solution)/shard_map/all_to_all | solution.py:97
  167.9 58.1 %copy-start.1 = (bf16[128,2048]{1,0:T(8,128)(2,1)S(1)}, bf16[128,2048]{1,0:T(8,128)(2,1)}, u32[]{:S(2)}) copy-start(bf16[128,2048]{1,0:T(8,128)(2,1)} %param.7) | copy-start | bytes 1572868
  213.1 58.1 %all-to-all-start.1 = ((bf16[16,12,2048]{2,1,0:T(8,128)(2,1)}), bf16[16,12,2048]{2,1,0:T(8,128)(2,1)S(1)}, u32[]{:S(2)}, u32[]{:S(2)}) async-start(bf16[16,12,2048]{2,1,0:T(8,128)(2,1)} %reshape.90), calls=%async_computation.1 | async-start | bytes 2097152 | tf_op jit(solution)/shard_map/all_to_all | solution.py:88
  271.5 6.0 %copy-start = (f32[128,2048]{1,0:T(8,128)S(1)}, f32[128,2048]{1,0:T(8,128)}, u32[]{:S(2)}) copy-start(f32[128,2048]{1,0:T(8,128)} %convert_element_type.44) | copy-start | bytes 3145732
Sparse Core Ops, SparseCore 0:
  11.1 70.1 all-gather.2
  84.4 59.5 all-gather.4
where the time goes:
time: 296 us; the launch traced here: 291 us
  waiting for transfers between devices  160 us (54%)
  starting transfers between devices  54.6 us (18%)
  local copies, waits for them, and re-layouts  31 us (10%)
  other arithmetic  16.3 us (6%)
  between operations  14.3 us (5%)
  matrix products  14.1 us (5%)
    all_to_all x1, waiting for transfers between devices, on_device(): lax.all_to_all(send_tokens, 'expert', split_axis=0, concat_axis=0, tiled=...  45.1 us
    all_to_all x1, waiting for transfers between devices, on_device(): lax.all_to_all(send_grads, 'expert', split_axis=0, concat_axis=0, tiled=T...  41.7 us
    all_to_all x1, waiting for transfers between devices, on_device(): lax.all_to_all(expert_grad.reshape(groups, capacity, width), 'expert', sp...  40.6 us
    all_to_all x1, waiting for transfers between devices, on_device(): lax.all_to_all(expert_out.reshape(groups, capacity, width), 'expert', spl...  31.7 us
    all_to_all x1, starting transfers between devices, on_device(): lax.all_to_all(send_grads, 'expert', split_axis=0, concat_axis=0, tiled=T...  15.7 us
    all_to_all x1, starting transfers between devices, on_device(): lax.all_to_all(send_tokens, 'expert', split_axis=0, concat_axis=0, tiled=...  13.2 us
    all_to_all x1, starting transfers between devices, on_device(): lax.all_to_all(expert_out.reshape(groups, capacity, width), 'expert', spl...  12.8 us
    all_to_all x1, starting transfers between devices, on_device(): lax.all_to_all(expert_grad.reshape(groups, capacity, width), 'expert', sp...  12.8 us
  transfers between devices with their start and end apart: 6, of which 4 were waited for; matrix products, arithmetic and copies ran while one was open for 14% of the time, Pallas kernels for 0%

commit v1 on v0

v1 whole, which is shorter than its diff:
```python
import functools

import jax
import jax.numpy as jnp
from jax import lax
from jax.experimental import pallas as pl
from jax.experimental.pallas import tpu as pltpu
from jax.sharding import PartitionSpec as P

MESH = pl.DeviceIdType.MESH
SLOTS = 16
GU_PIECE = 16
DN_PIECE = 32
NT = (((1,), (1,)), ((), ()))


def dot(a, b):
    return jnp.dot(a, b, preferred_element_type=jnp.float32)


def dot_nt(a, b):
    return lax.dot_general(a, b, NT, preferred_element_type=jnp.float32)


def rows_of(start, size):
    return pl.ds(pl.multiple_of(start, size), size)


def kernel(
    n,
    capacity,
    tokens,
    cotangent,
    routes,
    route_weights,
    gu_shard,
    dn_shard,
    mixed,
    grad_tokens,
    grad_gates,
    gu,
    dn,
    send_t,
    send_g,
    in_t,
    in_g,
    gate,
    up,
    hidden,
    ggu,
    out_s,
    eg_s,
    back_o,
    back_g,
    gu_recv,
    dn_recv,
    sib_gu,
    sib_dn,
    ring_send,
    sib_send,
    shard_send,
    row_recv,
    row_send,
    back_recv,
    back_send,
):
    tok_rows, width = tokens.shape
    top = routes.shape[1]
    shard = gu_shard.shape[1]
    ff = dn_shard.shape[2]
    slots = n * SLOTS
    sources = n
    half = width // 2
    gu_pieces = shard // GU_PIECE
    dn_pieces = shard // DN_PIECE
    me = lax.axis_index("fsdp")
    z = lax.axis_index("expert")
    q = me // 2
    core = lax.rem(me, 2)
    sibling = me + 1 - 2 * core
    after = lax.rem(z + 1 + core * (n - 2), n)
    before = lax.rem(z + n - 1 - core * (n - 2), n)
    passes_on = after != q

    barrier = pltpu.get_barrier_semaphore()

    def greet(k, carry):
        pl.semaphore_signal(
            barrier, inc=1, device_id=(lax.rem(me + k, 2 * n), z), device_id_type=MESH
        )
        return carry

    pl.semaphore_signal(barrier, inc=1, device_id=(me, after), device_id_type=MESH)
    pl.semaphore_signal(barrier, inc=1, device_id=(me, before), device_id_type=MESH)
    lax.fori_loop(1, 2 * n, greet, 0)

    lane = lax.broadcasted_iota(jnp.int32, (tok_rows, slots), 1)
    expert_of = lane // SLOTS
    slot_of = lane - expert_of * SLOTS
    weight_of = jnp.zeros((tok_rows, slots), jnp.float32)
    named = jnp.zeros((tok_rows, slots), jnp.float32)
    for k in range(top):
        hit = routes[:, k : k + 1] == expert_of
        named = jnp.where(hit, 1.0, named)
        weight_of = jnp.where(hit, route_weights[:, k : k + 1], weight_of)
    row_id = lax.broadcasted_iota(jnp.int32, (tok_rows, tok_rows), 0)
    col_id = lax.broadcasted_iota(jnp.int32, (tok_rows, tok_rows), 1)
    below = jnp.where(col_id < row_id, 1.0, 0.0).astype(jnp.bfloat16)
    earlier = dot(below, named.astype(jnp.bfloat16)).astype(jnp.int32)
    kept = (named > 0.5) & (earlier == slot_of) & (slot_of < capacity)
    chosen = jnp.where(kept, 1.0, 0.0)
    weight_of = jnp.where(kept, weight_of, 0.0)
    picks = jnp.transpose(chosen).astype(jnp.bfloat16)
    slot_weight = jnp.sum(jnp.transpose(weight_of), axis=1, keepdims=True)
    send_t[...] = dot(picks, tokens[...]).astype(jnp.bfloat16)
    send_g[...] = (slot_weight * dot(picks, cotangent[...])).astype(jnp.bfloat16)

    pl.semaphore_wait(barrier, 2 * n + 1)

    target = 2 * z + q // (n // 2)
    index = me - (q // (n // 2)) * sources

    def gu_piece(p):
        place = gu.at[rows_of(me * shard + p * GU_PIECE, GU_PIECE), :]
        return gu_shard.at[0, pl.ds(p * GU_PIECE, GU_PIECE), :], place, gu_recv.at[p * sources + index]

    def dn_piece(p):
        place = dn.at[rows_of(me * shard + p * DN_PIECE, DN_PIECE), :]
        return dn_shard.at[0, pl.ds(p * DN_PIECE, DN_PIECE), :], place, dn_recv.at[index * dn_pieces + p]

    shard_chunks = [gu_piece(p) for p in range(gu_pieces)] + [dn_piece(p) for p in range(dn_pieces)]

    @pl.when(target != me)
    def _():
        for source, place, sem in shard_chunks:
            pltpu.make_async_remote_copy(
                source, place, shard_send, sem, device_id=(target, z), device_id_type=MESH
            ).start()

    @pl.when(target == me)
    def _():
        for source, place, sem in shard_chunks:
            pltpu.make_async_copy(source, place, sem).start()

    mine = rows_of(q * SLOTS, SLOTS)

    def scatter_rows(source, place, send_sem, recv_sem):
        def step(k, carry):
            other = lax.rem(q + k, n)
            pltpu.make_async_remote_copy(
                source.at[rows_of(other * SLOTS, SLOTS), :],
                place.at[mine, :],
                send_sem,
                recv_sem,
                device_id=(2 * other + core, z),
                device_id_type=MESH,
            ).start()
            return carry

        pltpu.make_async_copy(source.at[mine, :], place.at[mine, :], recv_sem).start()
        lax.fori_loop(1, n, step, 0)

    def sent_rows(source, send_sem):
        rest = source.at[pl.ds(0, (n - 1) * SLOTS), :]
        pltpu.make_async_copy(rest, rest, send_sem).wait()

    def arrived_rows(place, recv_sem):
        pltpu.make_async_copy(place, place, recv_sem).wait()

    scatter_rows(send_t, in_t, row_send.at[0], row_recv.at[0])
    scatter_rows(send_g, in_g, row_send.at[1], row_recv.at[1])

    def pass_on(weight, start, size, recv_sem, sib_sem):
        chunk = weight.at[rows_of(start, size), :]
        pltpu.make_async_copy(chunk, chunk, recv_sem).wait()

        @pl.when(passes_on)
        def _():
            pltpu.make_async_remote_copy(
                chunk, chunk, ring_send, recv_sem, device_id=(me, after), device_id_type=MESH
            ).start()

        pltpu.make_async_remote_copy(
            chunk, chunk, sib_send, sib_sem, device_id=(sibling, z), device_id_type=MESH
        ).start()

    def gu_step(i, carry):
        p = i // sources
        s = i - p * sources
        start = core * half + s * shard + p * GU_PIECE
        pass_on(gu, start, GU_PIECE, gu_recv.at[i], sib_gu)
        return carry

    def dn_step(i, carry):
        pass_on(dn, core * half + i * DN_PIECE, DN_PIECE, dn_recv.at[i], sib_dn)
        return carry

    lax.fori_loop(0, gu_pieces * sources, gu_step, 0)
    lax.fori_loop(0, dn_pieces * sources, dn_step, 0)

    own = rows_of(core * half, half)
    theirs = rows_of((1 - core) * half, half)

    def wait_half(weight, sem, part):
        pltpu.make_async_copy(weight.at[part, :], weight.at[part, :], sem).wait()

    wait_half(gu, sib_gu, theirs)
    arrived_rows(in_t, row_recv.at[0])
    tile = min(256, ff)

    def gate_up_step(j, carry):
        cols = rows_of(j * tile, tile)
        gate[:, cols] = dot(in_t[...], gu[:, cols])
        up[:, cols] = dot(in_t[...], gu[:, rows_of(ff + j * tile, tile)])
        hidden[:, cols] = (jax.nn.silu(gate[:, cols]) * up[:, cols]).astype(jnp.bfloat16)
        return carry

    lax.fori_loop(0, ff // tile, gate_up_step, 0)
    wait_half(dn, sib_dn, theirs)

    def out_step(j, carry):
        cols = rows_of(j * tile, tile)
        out_s[:, cols] = dot_nt(hidden[...], dn[cols, :]).astype(jnp.bfloat16)
        return carry

    lax.fori_loop(0, width // tile, out_step, 0)
    scatter_rows(out_s, back_o, back_send.at[0], back_recv.at[0])

    arrived_rows(in_g, row_recv.at[1])

    def grad_hidden_step(j, carry):
        cols = rows_of(j * tile, tile)
        grad_hidden = dot(in_g[...], dn[:, cols])
        g = gate[:, cols]
        s = jax.nn.sigmoid(g)
        ggu[:, cols] = (grad_hidden * up[:, cols] * s * (1.0 + g * (1.0 - s))).astype(jnp.bfloat16)
        ggu[:, rows_of(ff + j * tile, tile)] = (grad_hidden * g * s).astype(jnp.bfloat16)
        return carry

    lax.fori_loop(0, ff // tile, grad_hidden_step, 0)

    def expert_grad_step(j, carry):
        cols = rows_of(j * tile, tile)
        eg_s[:, cols] = dot_nt(ggu[...], gu[cols, :]).astype(jnp.bfloat16)
        return carry

    lax.fori_loop(0, width // tile, expert_grad_step, 0)
    scatter_rows(eg_s, back_g, back_send.at[1], back_recv.at[1])

    @pl.when(passes_on)
    def _():
        wait_half(gu, ring_send, own)
        wait_half(dn, ring_send, own)

    wait_half(gu, sib_send, own)
    wait_half(dn, sib_send, own)

    @pl.when(target != me)
    def _():
        for weight in (gu, dn):
            part = weight.at[rows_of(me * shard, shard), :]
            pltpu.make_async_copy(part, part, shard_send).wait()

    sent_rows(send_t, row_send.at[0])
    sent_rows(send_g, row_send.at[1])

    first = weight_of.astype(jnp.bfloat16)
    rest = weight_of - first.astype(jnp.float32)
    second = rest.astype(jnp.bfloat16)
    third = (rest - second.astype(jnp.float32)).astype(jnp.bfloat16)
    chosen_half = chosen.astype(jnp.bfloat16)
    arrived_rows(back_o, back_recv.at[0])

    def mixed_step(j, products):
        cols = rows_of(j * tile, tile)
        out = back_o[:, cols]
        total = dot(first, out) + (dot(second, out) + dot(third, out))
        mixed[:, cols] = total.astype(jnp.bfloat16)
        return products + dot_nt(cotangent[:, cols], out)

    products = lax.fori_loop(
        0, width // tile, mixed_step, jnp.zeros((tok_rows, slots), jnp.float32)
    )
    products = jnp.where(kept, products, 0.0)
    for k in range(top):
        hit = routes[:, k : k + 1] == expert_of
        grad_gates[:, k : k + 1] = jnp.sum(jnp.where(hit, products, 0.0), axis=1, keepdims=True)

    arrived_rows(back_g, back_recv.at[1])

    def grad_step(j, carry):
        cols = rows_of(j * tile, tile)
        grad_tokens[:, cols] = dot(chosen_half, back_g[:, cols]).astype(jnp.bfloat16)
        return carry

    lax.fori_loop(0, width // tile, grad_step, 0)
    sent_rows(out_s, back_send.at[0])
    sent_rows(eg_s, back_send.at[1])


def on_device(tokens, cotangent, routes, route_weights, gate_up_weight, down_weight):
    n = lax.axis_size("expert")
    tok_rows, width = tokens.shape
    top = routes.shape[1]
    shard, ff = down_weight.shape[1:]
    capacity = 3 * tok_rows // 32
    slots = n * SLOTS
    rows = pltpu.VMEM((slots, width), jnp.bfloat16)
    gu_chunks = n * (shard // GU_PIECE)
    dn_chunks = n * (shard // DN_PIECE)
    dma = pltpu.SemaphoreType.DMA
    return pl.pallas_call(
        functools.partial(kernel, n, capacity),
        out_shape=(
            jax.ShapeDtypeStruct((tok_rows, width), jnp.bfloat16),
            jax.ShapeDtypeStruct((tok_rows, width), jnp.bfloat16),
            jax.ShapeDtypeStruct((tok_rows, top), jnp.float32),
        ),
        in_specs=[pl.BlockSpec(memory_space=pltpu.VMEM)] * 6,
        out_specs=[pl.BlockSpec(memory_space=pltpu.VMEM)] * 3,
        scratch_shapes=[
            pltpu.VMEM((width, 2 * ff), jnp.bfloat16),
            pltpu.VMEM((width, ff), jnp.bfloat16),
            rows,
            rows,
            rows,
            rows,
            pltpu.VMEM((slots, ff), jnp.float32),
            pltpu.VMEM((slots, ff), jnp.float32),
            pltpu.VMEM((slots, ff), jnp.bfloat16),
            pltpu.VMEM((slots, 2 * ff), jnp.bfloat16),
            rows,
            rows,
            rows,
            rows,
            dma((gu_chunks,)),
            dma((dn_chunks,)),
            dma,
            dma,
            dma,
            dma,
            dma,
            dma((2,)),
            dma((2,)),
            dma((2,)),
            dma((2,)),
        ],
        compiler_params=pltpu.CompilerParams(
            collective_id=0, has_side_effects=True, vmem_limit_bytes=44 * 1024 * 1024
        ),
    )(tokens, cotangent, routes, route_weights, gate_up_weight, down_weight)


def solution(mesh):
    rows = P(("fsdp", "expert"), None)
    weight = P("expert", "fsdp", None)
    return jax.shard_map(
        on_device,
        mesh=mesh,
        in_specs=(rows, rows, rows, rows, weight, weight),
        out_specs=(rows, rows, rows),
        check_vma=False,
    )
```

time: 296 us -> 203 us (0.69)
  the two profiles are of different devices: /device:TPU:1 before, /device:TPU:228 now
where the time goes in v1:
time: 203 us
  Pallas kernels  195 us (96%)
  local copies, waits for them, and re-layouts  6.86 us (3%)
    pallas_call x1, Pallas kernels, on_device(): pl.pallas_call(functools.partial(kernel, n, capacity), out_shape=(jax.Sha...  195 us
    unnamed x12, local copies, waits for them, and re-layouts  6.2 us

profile of v1, /device:TPU:228, one launch (start us, length us, event | category | flops | bytes accessed | tf_op | source)
XLA Modules:
  0.0 202.6 jit_solution(14350585246416933837)
XLA Ops:
  0.6 0.0 copy-start.3
  0.6 0.8 copy.9.routes
  1.5 0.8 copy.10.route_weights
  2.2 0.0 copy-done.3
  2.3 0.0 copy-start
  2.3 1.0 copy-done
  3.3 0.0 copy-start.1
  3.3 1.0 copy-done.1
  4.3 0.0 copy-start.2
  4.3 0.9 copy-done.2
  5.3 195.0 %shard_map.85 = (bf16[128,2048]{1,0:T(8,128)(2,1)S(1)}, bf16[128,2048]{1,0:T(8,128)(2,1)S(1)}, f32[128,8]{1,0:T(8,128)S(1)}) custom-call(bf16[128,2048]{1,0:T(8,128)(2,1)S(1)} %copy-done, bf16[128,2048]{1,0:T(8,128)(2,1)S(1)} %copy-done.1, s32[128,8]{1,0:T(8,128)S(1)} %copy.9.routes, f32[128,8]{1,0:T(8,128)S(1)} %copy.10.route_weights, ...), custom_call_target="tpu_custom_call" | custom-call | tf_op jit(solution)/shard_map/pallas_call | solution.py:312
  200.3 0.7 copy.11
  201.0 0.8 copy.14
  201.8 0.8 copy.15
Async XLA Ops:
  0.6 1.6 copy-start.3
  2.3 1.0 copy-start
  3.3 1.0 copy-start.1
  4.3 0.9 copy-start.2

commit v2 on v1

v2 whole, which is shorter than its diff:
```python
import functools

import jax
import jax.numpy as jnp
from jax import lax
from jax.experimental import pallas as pl
from jax.experimental.pallas import tpu as pltpu
from jax.sharding import PartitionSpec as P

MESH = pl.DeviceIdType.MESH
SLOTS = 16
GU_PIECE = 16
DN_PIECE = 32
GU_CHUNKS = 64
CHUNKS = 3 * GU_CHUNKS
MEET_FIRST, MEET_STEP = 132, 5
GU_LEAD, DN_LEAD = 5, 20
HOP, SLACK = 6, 8
T_CALL, G_CALL = 70, 100
NT = (((1,), (1,)), ((), ()))


def dot(a, b):
    return jnp.dot(a, b, preferred_element_type=jnp.float32)


def dot_nt(a, b):
    return lax.dot_general(a, b, NT, preferred_element_type=jnp.float32)


def rows_of(start, size):
    return pl.ds(pl.multiple_of(start, size), size)


def nearest_row(q, h):
    y = q // 4
    a = lax.rem(2 * h - y + 4, 4)
    b = lax.rem(2 * h + 1 - y + 4, 4)
    return jnp.where(jnp.minimum(a, 4 - a) <= jnp.minimum(b, 4 - b), 2 * h, 2 * h + 1)


def device_at(q, h, near, j):
    k = j // 2
    row = jnp.where(k < 4, near, 4 * h + 1 - near)
    d = lax.rem(k, 4)
    x = lax.rem(lax.rem(q, 4) + d + jnp.where(d == 2, 1, 0) - jnp.where(d == 3, 1, 0), 4)
    return 2 * (4 * row + x) + lax.rem(j, 2)


def rank_of(q, f):
    c = f // 2
    near = nearest_row(q, c // 8)
    off = lax.rem(lax.rem(c, 4) - lax.rem(q, 4) + 4, 4)
    d = off - jnp.where(off == 3, 1, 0) + jnp.where(off == 2, 1, 0)
    return 2 * (jnp.where(c // 4 == near, 0, 4) + d) + lax.rem(f, 2)


def kernel(
    n,
    capacity,
    tokens_hbm,
    cotangent_hbm,
    routes,
    route_weights,
    gu_shard,
    dn_shard,
    mixed,
    grad_tokens,
    grad_gates,
    tokens,
    cotangent,
    gu,
    dn,
    send_t,
    send_g,
    in_t,
    in_g,
    gate,
    up,
    hidden,
    ggu,
    out_s,
    eg_s,
    back_o,
    back_g,
    load,
    ring,
    sib,
    ring_send,
    sib_send,
    shard_send,
    row_recv,
    row_send,
    back_recv,
    back_send,
    go,
):
    tok_rows, width = tokens.shape
    top = routes.shape[0]
    shard = gu_shard.shape[1]
    ff = dn_shard.shape[2]
    slots = n * SLOTS
    me = lax.axis_index("fsdp")
    z = lax.axis_index("expert")
    q = me // 2
    core = lax.rem(me, 2)
    sibling = me + 1 - 2 * core
    upward = core == 0
    after = lax.rem(z + 1 + core * (n - 2), n)
    before = lax.rem(z + n - 1 - core * (n - 2), n)

    loads = (
        pltpu.make_async_copy(tokens_hbm, tokens, load.at[0]),
        pltpu.make_async_copy(cotangent_hbm, cotangent, load.at[1]),
    )
    for copy in loads:
        copy.start()

    barrier = pltpu.get_barrier_semaphore()

    def greet(k, carry):
        pl.semaphore_signal(
            barrier, inc=1, device_id=(lax.rem(me + k, 2 * n), z), device_id_type=MESH
        )
        return carry

    pl.semaphore_signal(barrier, inc=1, device_id=(me, after), device_id_type=MESH)
    pl.semaphore_signal(barrier, inc=1, device_id=(me, before), device_id_type=MESH)
    lax.fori_loop(1, 2 * n, greet, 0)

    slot_id = lax.broadcasted_iota(jnp.int32, (slots, tok_rows), 0)
    expert_of = slot_id // SLOTS
    slot_of = slot_id - expert_of * SLOTS
    weight_of = jnp.zeros((slots, tok_rows), jnp.float32)
    named = jnp.zeros((slots, tok_rows), jnp.float32)
    for k in range(top):
        hit = routes[k : k + 1, :] == expert_of
        named = jnp.where(hit, 1.0, named)
        weight_of = jnp.where(hit, route_weights[k : k + 1, :], weight_of)
    row_id = lax.broadcasted_iota(jnp.int32, (tok_rows, tok_rows), 0)
    col_id = lax.broadcasted_iota(jnp.int32, (tok_rows, tok_rows), 1)
    above = jnp.where(row_id < col_id, 1.0, 0.0).astype(jnp.bfloat16)
    earlier = dot(named.astype(jnp.bfloat16), above).astype(jnp.int32)
    kept = (named > 0.5) & (earlier == slot_of) & (slot_of < capacity)
    chosen = jnp.where(kept, 1.0, 0.0)
    weight_of = jnp.where(kept, weight_of, 0.0)
    picks = chosen.astype(jnp.bfloat16)
    slot_weight = jnp.sum(weight_of, axis=1, keepdims=True)
    loads[0].wait()
    send_t[...] = dot(picks, tokens[...]).astype(jnp.bfloat16)
    loads[1].wait()
    send_g[...] = (slot_weight * dot(picks, cotangent[...])).astype(jnp.bfloat16)

    pl.semaphore_wait(barrier, 2 * n + 1)

    def meet(d):
        return jnp.minimum(jnp.maximum(8 * ((MEET_FIRST - MEET_STEP * d + 4) // 8), GU_CHUNKS), 2 * GU_CHUNKS)

    d = lax.rem(z - q + n, n)
    dist = jnp.where(upward, d, lax.rem(n - d, n))
    next_d = jnp.where(upward, d + 1, lax.rem(d + n - 1, n))
    is_first = d == 0
    own = jnp.where(is_first, CHUNKS // 2, jnp.where(upward, meet(d), CHUNKS - meet(d)))
    passed = jnp.where(upward, meet(next_d), CHUNKS - meet(next_d))
    passed = jnp.where((next_d == 0) | (next_d == n), 0, passed)

    def number(u):
        return jnp.where(upward, u, CHUNKS - 1 - u)

    half_me = q // (n // 2)
    target = 2 * z + half_me
    rank = rank_of(z, me)
    is_remote = target != me

    def place_in_order(t):
        return jnp.where(half_me == 0, t, CHUNKS - 1 - t)

    def gu_shard_chunks():
        for p in range(shard // GU_PIECE):
            yield (
                gu_shard.at[0, pl.ds(p * GU_PIECE, GU_PIECE), :],
                gu.at[rows_of(me * shard + p * GU_PIECE, GU_PIECE), :],
                ring.at[place_in_order(4 * rank + p)],
            )

    def dn_shard_chunks():
        for p in range(shard // DN_PIECE):
            yield (
                dn_shard.at[0, pl.ds(p * DN_PIECE, DN_PIECE), :],
                dn.at[rows_of(me * shard + p * DN_PIECE, DN_PIECE), :],
                ring.at[place_in_order(GU_CHUNKS + 2 * rank + p)],
            )

    def send_shard(chunks, k):
        for source, place, sem in chunks():
            pltpu.make_async_remote_copy(
                source, place, shard_send.at[k], sem, device_id=(target, z), device_id_type=MESH
            ).start()

    def send_shard_on_call(chunks, k):
        pl.semaphore_wait(go.at[k], 1)
        send_shard(chunks, k)

    at_once = rank < GU_LEAD
    gu_call = 4 * (rank - GU_LEAD) - HOP * dist + SLACK
    dn_call = GU_CHUNKS + 2 * rank - DN_LEAD - HOP * dist + SLACK

    @pl.when(jnp.logical_not(is_remote))
    def _():
        for chunks in (gu_shard_chunks, dn_shard_chunks):
            for source, place, sem in chunks():
                pltpu.make_async_copy(source, place, sem).start()

    @pl.when(is_remote & at_once)
    def _():
        send_shard(gu_shard_chunks, 0)

    @pl.when(is_remote & jnp.logical_not(at_once) & (gu_call < 0))
    def _():
        send_shard_on_call(gu_shard_chunks, 0)

    @pl.when(is_remote & (dn_call < 0))
    def _():
        send_shard_on_call(dn_shard_chunks, 1)

    gu_call = jnp.where(is_remote & jnp.logical_not(at_once), gu_call, -1)
    dn_call = jnp.where(is_remote, dn_call, -1)

    mine = rows_of(q * SLOTS, SLOTS)

    def scatter_rows(source, place, send_sem, recv_sem):
        def step(k, carry):
            other = lax.rem(q + k, n)
            pltpu.make_async_remote_copy(
                source.at[rows_of(other * SLOTS, SLOTS), :],
                place.at[mine, :],
                send_sem,
                recv_sem,
                device_id=(2 * other + core, z),
                device_id_type=MESH,
            ).start()
            return carry

        pltpu.make_async_copy(source.at[mine, :], place.at[mine, :], recv_sem).start()
        lax.fori_loop(1, n, step, 0)

    def sent_rows(source, send_sem):
        rest = source.at[pl.ds(0, (n - 1) * SLOTS), :]
        pltpu.make_async_copy(rest, rest, send_sem).wait()

    def arrived_rows(place, recv_sem):
        pltpu.make_async_copy(place, place, recv_sem).wait()

    t_call = jnp.maximum(T_CALL - HOP * dist, 0)
    g_call = jnp.minimum(jnp.maximum(G_CALL - HOP * dist, 1), own - 1)

    near = (nearest_row(q, 0), nearest_row(q, 1))

    def half_of(u):
        i = number(u)
        h = jnp.where(i < CHUNKS // 2, 0, 1)
        t = jnp.where(h == 0, i, CHUNKS - 1 - i)
        return h, t, jnp.where(h == 0, near[0], near[1])

    def gu_chunk(u):
        h, t, row = half_of(u)
        start = device_at(q, h, row, t // 4) * shard + lax.rem(t, 4) * GU_PIECE
        return gu.at[rows_of(start, GU_PIECE), :]

    def dn_chunk(u):
        h, t, row = half_of(u)
        t = t - GU_CHUNKS
        start = device_at(q, h, row, t // 2) * shard + lax.rem(t, 2) * DN_PIECE
        return dn.at[rows_of(start, DN_PIECE), :]

    def pass_on(chunk, u):
        i = number(u)

        @pl.when(u < passed)
        def _():
            pltpu.make_async_remote_copy(
                chunk, chunk, ring_send.at[i // 8], ring.at[i], device_id=(me, after), device_id_type=MESH
            ).start()

    def take(chunk, u):
        i = number(u)
        pltpu.make_async_copy(chunk, chunk, ring.at[i]).wait()
        pass_on(chunk, u)
        pltpu.make_async_remote_copy(
            chunk, chunk, sib_send.at[i // 8], sib.at[i // 8], device_id=(sibling, z), device_id_type=MESH
        ).start()

    def call_shards(u):
        def call(j, k):
            f = device_at(q, core, jnp.where(upward, near[0], near[1]), j)

            @pl.when(f != me)
            def _():
                pl.semaphore_signal(go.at[k], inc=1, device_id=(f, z), device_id_type=MESH)

        j = u // 4 + GU_LEAD
        k = (u - GU_CHUNKS + DN_LEAD) // 2

        @pl.when(is_first & (lax.rem(u, 4) == 0) & (j < n))
        def _():
            call(j, 0)

        @pl.when(is_first & (lax.rem(u, 2) == 0) & (u >= GU_CHUNKS - DN_LEAD) & (k < n))
        def _():
            call(k, 1)

    def beside(u):
        call_shards(u)

        @pl.when(u == gu_call)
        def _():
            send_shard_on_call(gu_shard_chunks, 0)

        @pl.when(u == dn_call)
        def _():
            send_shard_on_call(dn_shard_chunks, 1)

        @pl.when(u == t_call)
        def _():
            scatter_rows(send_t, in_t, row_send.at[0], row_recv.at[0])

        @pl.when(u == g_call)
        def _():
            scatter_rows(send_g, in_g, row_send.at[1], row_recv.at[1])

    def gu_step(u, carry):
        beside(u)
        take(gu_chunk(u), u)
        return carry

    def dn_step(u, carry):
        beside(u)
        take(dn_chunk(u), u)
        return carry

    lax.fori_loop(0, GU_CHUNKS, gu_step, 0)
    lax.fori_loop(GU_CHUNKS, own, dn_step, 0)

    def wait_group(g, sems):
        group = gu.at[pl.ds(0, 8 * GU_PIECE), :]
        pltpu.make_async_copy(group, group, sems.at[number(8 * g) // 8]).wait()

    def group_step(g, carry):
        wait_group(g, sib)

        def one(k, carry):
            pass_on(dn_chunk(8 * g + k), 8 * g + k)
            return carry

        lax.fori_loop(0, 8, one, 0)
        return carry

    def wait_step(g, carry):
        wait_group(g, sib)
        return carry

    seen = jnp.maximum(own, passed) // 8
    lax.fori_loop(own // 8, seen, group_step, 0)
    lax.fori_loop(2 * GU_CHUNKS // 8, CHUNKS // 8, wait_step, 0)

    arrived_rows(in_t, row_recv.at[0])
    tile = min(256, ff)

    def gate_up_step(j, carry):
        cols = rows_of(j * tile, tile)
        gate[:, cols] = dot(in_t[...], gu[:, cols])
        up[:, cols] = dot(in_t[...], gu[:, rows_of(ff + j * tile, tile)])
        hidden[:, cols] = (jax.nn.silu(gate[:, cols]) * up[:, cols]).astype(jnp.bfloat16)
        return carry

    lax.fori_loop(0, ff // tile, gate_up_step, 0)
    lax.fori_loop(seen, 2 * GU_CHUNKS // 8, wait_step, 0)

    def out_step(j, carry):
        cols = rows_of(j * tile, tile)
        out_s[:, cols] = dot_nt(hidden[...], dn[cols, :]).astype(jnp.bfloat16)
        return carry

    lax.fori_loop(0, width // tile, out_step, 0)
    scatter_rows(out_s, back_o, back_send.at[0], back_recv.at[0])

    arrived_rows(in_g, row_recv.at[1])

    def grad_hidden_step(j, carry):
        cols = rows_of(j * tile, tile)
        grad_hidden = dot(in_g[...], dn[:, cols])
        g = gate[:, cols]
        s = jax.nn.sigmoid(g)
        ggu[:, cols] = (grad_hidden * up[:, cols] * s * (1.0 + g * (1.0 - s))).astype(jnp.bfloat16)
        ggu[:, rows_of(ff + j * tile, tile)] = (grad_hidden * g * s).astype(jnp.bfloat16)
        return carry

    lax.fori_loop(0, ff // tile, grad_hidden_step, 0)

    def expert_grad_step(j, carry):
        cols = rows_of(j * tile, tile)
        eg_s[:, cols] = dot_nt(ggu[...], gu[cols, :]).astype(jnp.bfloat16)
        return carry

    lax.fori_loop(0, width // tile, expert_grad_step, 0)
    scatter_rows(eg_s, back_g, back_send.at[1], back_recv.at[1])

    def ring_sent(g, carry):
        wait_group(g, ring_send)
        return carry

    def sib_sent(g, carry):
        wait_group(g, sib_send)
        return carry

    lax.fori_loop(0, passed // 8, ring_sent, 0)
    lax.fori_loop(0, own // 8, sib_sent, 0)

    @pl.when(is_remote)
    def _():
        for k, weight in enumerate((gu, dn)):
            part = weight.at[rows_of(me * shard, shard), :]
            pltpu.make_async_copy(part, part, shard_send.at[k]).wait()

    sent_rows(send_t, row_send.at[0])
    sent_rows(send_g, row_send.at[1])

    by_token = jnp.transpose(weight_of)
    first = by_token.astype(jnp.bfloat16)
    rest = by_token - first.astype(jnp.float32)
    second = rest.astype(jnp.bfloat16)
    third = (rest - second.astype(jnp.float32)).astype(jnp.bfloat16)
    chosen_by_token = jnp.transpose(chosen).astype(jnp.bfloat16)
    arrived_rows(back_o, back_recv.at[0])

    def mixed_step(j, products):
        cols = rows_of(j * tile, tile)
        out = back_o[:, cols]
        total = dot(first, out) + (dot(second, out) + dot(third, out))
        mixed[:, cols] = total.astype(jnp.bfloat16)
        return products + dot_nt(out, cotangent[:, cols])

    products = lax.fori_loop(
        0, width // tile, mixed_step, jnp.zeros((slots, tok_rows), jnp.float32)
    )
    products = jnp.where(kept, products, 0.0)
    for k in range(top):
        hit = routes[k : k + 1, :] == expert_of
        grad_gates[k : k + 1, :] = jnp.sum(jnp.where(hit, products, 0.0), axis=0, keepdims=True)

    arrived_rows(back_g, back_recv.at[1])

    def grad_step(j, carry):
        cols = rows_of(j * tile, tile)
        grad_tokens[:, cols] = dot(chosen_by_token, back_g[:, cols]).astype(jnp.bfloat16)
        return carry

    lax.fori_loop(0, width // tile, grad_step, 0)
    sent_rows(out_s, back_send.at[0])
    sent_rows(eg_s, back_send.at[1])


def on_device(tokens, cotangent, routes, route_weights, gate_up_weight, down_weight):
    n = lax.axis_size("expert")
    tok_rows, width = tokens.shape
    top = routes.shape[1]
    shard, ff = down_weight.shape[1:]
    capacity = 3 * tok_rows // 32
    slots = n * SLOTS
    rows = pltpu.VMEM((slots, width), jnp.bfloat16)
    dma = pltpu.SemaphoreType.DMA
    hbm = pl.BlockSpec(memory_space=pl.ANY)
    vmem = pl.BlockSpec(memory_space=pltpu.VMEM)
    mixed, grad_tokens, grad_gates = pl.pallas_call(
        functools.partial(kernel, n, capacity),
        out_shape=(
            jax.ShapeDtypeStruct((tok_rows, width), jnp.bfloat16),
            jax.ShapeDtypeStruct((tok_rows, width), jnp.bfloat16),
            jax.ShapeDtypeStruct((top, tok_rows), jnp.float32),
        ),
        in_specs=[hbm, hbm, vmem, vmem, hbm, hbm],
        out_specs=[vmem] * 3,
        scratch_shapes=[
            pltpu.VMEM((tok_rows, width), jnp.bfloat16),
            pltpu.VMEM((tok_rows, width), jnp.bfloat16),
            pltpu.VMEM((width, 2 * ff), jnp.bfloat16),
            pltpu.VMEM((width, ff), jnp.bfloat16),
            rows,
            rows,
            rows,
            rows,
            pltpu.VMEM((slots, ff), jnp.float32),
            pltpu.VMEM((slots, ff), jnp.float32),
            pltpu.VMEM((slots, ff), jnp.bfloat16),
            pltpu.VMEM((slots, 2 * ff), jnp.bfloat16),
            rows,
            rows,
            rows,
            rows,
            dma((2,)),
            dma((CHUNKS,)),
            dma((CHUNKS // 8,)),
            dma((CHUNKS // 8,)),
            dma((CHUNKS // 8,)),
            dma((2,)),
            dma((2,)),
            dma((2,)),
            dma((2,)),
            dma((2,)),
            pltpu.SemaphoreType.REGULAR((2,)),
        ],
        compiler_params=pltpu.CompilerParams(
            collective_id=0, has_side_effects=True, vmem_limit_bytes=56 * 1024 * 1024
        ),
    )(tokens, cotangent, routes.T, route_weights.T, gate_up_weight, down_weight)
    return mixed, grad_tokens, grad_gates.T


def solution(mesh):
    rows = P(("fsdp", "expert"), None)
    weight = P("expert", "fsdp", None)
    return jax.shard_map(
        on_device,
        mesh=mesh,
        in_specs=(rows, rows, rows, rows, weight, weight),
        out_specs=(rows, rows, rows),
        check_vma=False,
    )
```

time: 203 us -> 166 us (0.82)
  the two profiles are of different devices: /device:TPU:228 before, /device:TPU:1 now
where the time goes in v2:
time: 166 us; the launch traced here: 165 us
  Pallas kernels  161 us (97%)
  local copies, waits for them, and re-layouts  3.33 us (2%)
    pallas_call x1, Pallas kernels, on_device(): pl.pallas_call(functools.partial(kernel, n, capacity), out_shape=(jax.Sha...  161 us
    unnamed x7, local copies, waits for them, and re-layouts  3.33 us

profile of v2, /device:TPU:1, one launch (start us, length us, event | category | flops | bytes accessed | tf_op | source)
XLA Modules:
  0.0 164.8 jit_solution(14602968722413150567)
XLA Ops:
  0.6 160.8 %shard_map.85 = (bf16[128,2048]{1,0:T(8,128)(2,1)}, bf16[128,2048]{1,0:T(8,128)(2,1)}, f32[8,128]{1,0:T(8,128)}) custom-call(bf16[128,2048]{1,0:T(8,128)(2,1)} %tokens_hbm.1, bf16[128,2048]{1,0:T(8,128)(2,1)} %cotangent_hbm.1, s32[8,128]{1,0:T(8,128)} %bitcast.3, f32[8,128]{1,0:T(8,128)} %bitcast.4, bf16[1,64,1536]{2,1,0:T(8,128)(2,1)} %gu_shard.1, ...), custom_call_target="tpu_custom_call" | custom-call | tf_op jit(solution)/shard_map/pallas_call | solution.py:474
  161.4 0.0 copy-start
  161.4 1.9 %copy.12 = bf16[128,2048]{1,0:T(8,128)(2,1)} copy(bf16[128,2048]{1,0:T(8,128)(2,1)} %get-tuple-element.12) | data formatting | bytes 1048576
  163.4 0.0 copy-done
  163.4 0.0 copy-start.1
  163.4 0.8 copy.13
  164.2 0.0 copy-done.1
  164.2 0.6 copy.14
Async XLA Ops:
  161.4 2.0 %copy-start = (bf16[128,2048]{1,0:T(8,128)(2,1)S(1)}, bf16[128,2048]{1,0:T(8,128)(2,1)}, u32[]{:S(2)}) copy-start(bf16[128,2048]{1,0:T(8,128)(2,1)} %get-tuple-element.13) | copy-start | bytes 1572868
  163.4 0.8 copy-start.1

commit v3 on v2

v3 whole, which is shorter than its diff:
```python
import functools

import jax
import jax.numpy as jnp
from jax import lax
from jax.experimental import pallas as pl
from jax.experimental.pallas import tpu as pltpu
from jax.sharding import PartitionSpec as P

MESH = pl.DeviceIdType.MESH
SLOTS = 16
GU_PIECE = 16
DN_PIECE = 32
GU_CHUNKS = 64
CHUNKS = 3 * GU_CHUNKS
MEET_FIRST, MEET_STEP = 130, 5
GU_LEAD, DN_LEAD = 5, 20
HOP, SLACK = 6, 8
ROW_CALL, ROW_EVERY = 110, 2
OTHER_UP, OTHER_DOWN, OTHER_STEP = 77, 98, 11
MARGIN = 10
WIDE = 512
NT = (((1,), (1,)), ((), ()))


def dot(a, b):
    return jnp.dot(a, b, preferred_element_type=jnp.float32)


def dot_nt(a, b):
    return lax.dot_general(a, b, NT, preferred_element_type=jnp.float32)


def rows_of(start, size):
    return pl.ds(pl.multiple_of(start, size), size)


def nearest_row(q, h):
    y = q // 4
    a = lax.rem(2 * h - y + 4, 4)
    b = lax.rem(2 * h + 1 - y + 4, 4)
    return jnp.where(jnp.minimum(a, 4 - a) <= jnp.minimum(b, 4 - b), 2 * h, 2 * h + 1)


def chip_at(q, r):
    k = r // 2
    h = jnp.where(lax.rem(r, 2) == 0, q // 8, 1 - q // 8)
    near = nearest_row(q, h)
    row = jnp.where(k < 4, near, 4 * h + 1 - near)
    d = lax.rem(k, 4)
    x = lax.rem(lax.rem(q, 4) + d + jnp.where(d == 2, 1, 0) - jnp.where(d == 3, 1, 0), 4)
    return 4 * row + x


def rank_of(q, c):
    near = nearest_row(q, c // 8)
    off = lax.rem(lax.rem(c, 4) - lax.rem(q, 4) + 4, 4)
    d = off - jnp.where(off == 3, 1, 0) + jnp.where(off == 2, 1, 0)
    return 2 * (jnp.where(c // 4 == near, 0, 4) + d) + jnp.where(c // 8 == q // 8, 0, 1)


def is_opposite(q, c):
    return (lax.rem(c // 4 - q // 4 + 4, 4) == 2) & (lax.rem(c, 4) != lax.rem(q, 4))


def kernel(
    n,
    capacity,
    tokens_hbm,
    cotangent_hbm,
    routes,
    route_weights,
    gu_shard,
    dn_shard,
    mixed,
    back_g,
    by_slot,
    grad_gates,
    tokens,
    cotangent,
    gu,
    dn,
    send_t,
    send_g,
    in_t,
    in_g,
    gate,
    up,
    hidden,
    ggu,
    out_s,
    eg_s,
    back_o,
    gu_other,
    dn_other,
    load,
    ring,
    sib,
    ring_send,
    sib_send,
    shard_send,
    row_recv,
    row_send,
    back_recv,
    back_send,
    other_recv,
    go,
):
    tok_rows, width = tokens.shape
    top = routes.shape[0]
    shard = gu_shard.shape[1]
    ff = dn_shard.shape[2]
    slots = n * SLOTS
    me = lax.axis_index("fsdp")
    z = lax.axis_index("expert")
    q = me // 2
    core = lax.rem(me, 2)
    sibling = me + 1 - 2 * core
    upward = core == 0
    after = lax.rem(z + 1 + core * (n - 2), n)
    before = lax.rem(z + n - 1 - core * (n - 2), n)

    loads = (
        pltpu.make_async_copy(tokens_hbm, tokens, load.at[0]),
        pltpu.make_async_copy(cotangent_hbm, cotangent, load.at[1]),
    )
    for copy in loads:
        copy.start()

    barrier = pltpu.get_barrier_semaphore()

    def greet(k, carry):
        pl.semaphore_signal(
            barrier, inc=1, device_id=(lax.rem(me + k, 2 * n), z), device_id_type=MESH
        )
        return carry

    pl.semaphore_signal(barrier, inc=1, device_id=(me, after), device_id_type=MESH)
    pl.semaphore_signal(barrier, inc=1, device_id=(me, before), device_id_type=MESH)
    lax.fori_loop(1, 2 * n, greet, 0)

    slot_id = lax.broadcasted_iota(jnp.int32, (slots, tok_rows), 0)
    expert_of = slot_id // SLOTS
    slot_of = slot_id - expert_of * SLOTS
    weight_of = jnp.zeros((slots, tok_rows), jnp.float32)
    named = jnp.zeros((slots, tok_rows), jnp.float32)
    for k in range(top):
        hit = routes[k : k + 1, :] == expert_of
        named = jnp.where(hit, 1.0, named)
        weight_of = jnp.where(hit, route_weights[k : k + 1, :], weight_of)
    row_id = lax.broadcasted_iota(jnp.int32, (tok_rows, tok_rows), 0)
    col_id = lax.broadcasted_iota(jnp.int32, (tok_rows, tok_rows), 1)
    above = jnp.where(row_id < col_id, 1.0, 0.0).astype(jnp.bfloat16)
    earlier = dot(named.astype(jnp.bfloat16), above).astype(jnp.int32)
    kept = (named > 0.5) & (earlier == slot_of) & (slot_of < capacity)
    chosen = jnp.where(kept, 1.0, 0.0)
    weight_of = jnp.where(kept, weight_of, 0.0)
    picks = chosen.astype(jnp.bfloat16)
    slot_weight = jnp.sum(weight_of, axis=1, keepdims=True)
    loads[0].wait()
    send_t[...] = dot(picks, tokens[...]).astype(jnp.bfloat16)
    loads[1].wait()
    send_g[...] = (slot_weight * dot(picks, cotangent[...])).astype(jnp.bfloat16)

    pl.semaphore_wait(barrier, 2 * n + 1)

    def meet(d):
        return jnp.minimum(jnp.maximum(8 * ((MEET_FIRST - MEET_STEP * d + 4) // 8), GU_CHUNKS), 2 * GU_CHUNKS)

    d = lax.rem(z - q + n, n)
    dist = jnp.where(upward, d, lax.rem(n - d, n))
    next_d = jnp.where(upward, d + 1, lax.rem(d + n - 1, n))
    is_first = d == 0
    own = jnp.where(is_first, CHUNKS // 2, jnp.where(upward, meet(d), CHUNKS - meet(d)))
    passed = jnp.where(upward, meet(next_d), CHUNKS - meet(next_d))
    passed = jnp.where((next_d == 0) | (next_d == n), 0, passed)

    def number(u):
        return jnp.where(upward, u, CHUNKS - 1 - u)

    is_target = q == z
    opposite = lax.rem(q + n // 2, n)
    goes_by = is_opposite(z, q)
    is_between = is_opposite(z, opposite)
    between = 4 * (z // 4) + lax.rem(q, 4)

    def place_in_order(t):
        return jnp.where(upward, t, CHUNKS - 1 - t)

    def shard_chunks(part, source, chip):
        owner, rank = 2 * chip + core, rank_of(z, chip)
        size, weight, at = ((GU_PIECE, gu, 4 * rank), (DN_PIECE, dn, GU_CHUNKS + 2 * rank))[part]
        for p in range(shard // size):
            yield (
                source.at[pl.ds(p * size, size), :],
                weight.at[rows_of(owner * shard + p * size, size), :],
                ring.at[place_in_order(at + p)],
            )

    shards = (gu_shard.at[0], dn_shard.at[0])
    others = (gu_other, dn_other)

    def send_shard(part):
        for source, place, sem in shard_chunks(part, shards[part], q):
            pltpu.make_async_remote_copy(
                source, place, shard_send.at[part], sem, device_id=(2 * z + core, z), device_id_type=MESH
            ).start()

    def send_shard_on_call(part):
        pl.semaphore_wait(go.at[part], 1)
        send_shard(part)

    def send_other_on_call(part):
        pltpu.make_async_copy(others[part], others[part], other_recv.at[part]).wait()
        pl.semaphore_wait(go.at[2 + part], 1)
        for source, place, sem in shard_chunks(part, others[part], opposite):
            pltpu.make_async_remote_copy(
                source, place, shard_send.at[2 + part], sem, device_id=(2 * z + core, z), device_id_type=MESH
            ).start()

    def calls(rank):
        gu_call = 4 * (rank - GU_LEAD) - HOP * dist + SLACK
        dn_call = GU_CHUNKS + 2 * rank - DN_LEAD - HOP * dist + SLACK
        return gu_call, dn_call

    rank = rank_of(z, q)
    at_once = rank < GU_LEAD
    is_direct = jnp.logical_not(is_target | goes_by)
    gu_call, dn_call = calls(rank)
    gu_other_call, dn_other_call = calls(rank_of(z, opposite))

    @pl.when(is_target)
    def _():
        for part in range(2):
            for source, place, sem in shard_chunks(part, shards[part], q):
                pltpu.make_async_copy(source, place, sem).start()

    @pl.when(goes_by)
    def _():
        for part in range(2):
            pltpu.make_async_remote_copy(
                shards[part],
                others[part],
                shard_send.at[part],
                other_recv.at[part],
                device_id=(2 * between + core, z),
                device_id_type=MESH,
            ).start()

    @pl.when(is_direct & at_once)
    def _():
        send_shard(0)

    @pl.when(is_direct & jnp.logical_not(at_once) & (gu_call < 0))
    def _():
        send_shard_on_call(0)

    @pl.when(is_between & (gu_other_call < 0))
    def _():
        send_other_on_call(0)

    @pl.when(is_direct & (dn_call < 0))
    def _():
        send_shard_on_call(1)

    @pl.when(is_between & (dn_other_call < 0))
    def _():
        send_other_on_call(1)

    gu_call = jnp.where(is_direct & jnp.logical_not(at_once), gu_call, -1)
    dn_call = jnp.where(is_direct, dn_call, -1)
    gu_other_call = jnp.where(is_between, gu_other_call, -1)
    dn_other_call = jnp.where(is_between, dn_other_call, -1)

    mine = rows_of(q * SLOTS, SLOTS)

    def keep_rows(source, place, recv_sem):
        pltpu.make_async_copy(source.at[mine, :], place.at[mine, :], recv_sem).start()

    def send_rows(k, source, place, send_sem, recv_sem):
        other = lax.rem(q + k, n)
        pltpu.make_async_remote_copy(
            source.at[rows_of(other * SLOTS, SLOTS), :],
            place.at[mine, :],
            send_sem,
            recv_sem,
            device_id=(2 * other + core, z),
            device_id_type=MESH,
        ).start()

    def scatter_rows(source, place, send_sem, recv_sem):
        def step(k, carry):
            send_rows(k, source, place, send_sem, recv_sem)
            return carry

        keep_rows(source, place, recv_sem)
        lax.fori_loop(1, n, step, 0)

    def sent_rows(source, send_sem):
        rest = source.at[pl.ds(0, (n - 1) * SLOTS), :]
        pltpu.make_async_copy(rest, rest, send_sem).wait()

    def arrived_rows(place, recv_sem):
        pltpu.make_async_copy(place, place, recv_sem).wait()

    keep_rows(send_t, in_t, row_recv.at[0])
    keep_rows(send_g, in_g, row_recv.at[1])
    row_call = jnp.minimum(jnp.maximum(ROW_CALL - HOP * dist, 0), own - 2 * ROW_EVERY * (n - 1))

    def gu_chunk(u):
        i = number(u)
        h = jnp.where(i < CHUNKS // 2, 0, 1)
        t = jnp.where(h == 0, i, CHUNKS - 1 - i)
        start = (2 * chip_at(q, t // 4) + h) * shard + lax.rem(t, 4) * GU_PIECE
        return gu.at[rows_of(start, GU_PIECE), :]

    def dn_chunk(u):
        i = number(u)
        h = jnp.where(i < CHUNKS // 2, 0, 1)
        t = jnp.where(h == 0, i, CHUNKS - 1 - i) - GU_CHUNKS
        start = (2 * chip_at(q, t // 2) + h) * shard + lax.rem(t, 2) * DN_PIECE
        return dn.at[rows_of(start, DN_PIECE), :]

    def pass_on(chunk, u):
        i = number(u)

        @pl.when(u < passed)
        def _():
            pltpu.make_async_remote_copy(
                chunk, chunk, ring_send.at[i // 8], ring.at[i], device_id=(me, after), device_id_type=MESH
            ).start()

    def take(chunk, u):
        i = number(u)
        pltpu.make_async_copy(chunk, chunk, ring.at[i]).wait()
        pass_on(chunk, u)
        pltpu.make_async_remote_copy(
            chunk, chunk, sib_send.at[i // 8], sib.at[i // 8], device_id=(sibling, z), device_id_type=MESH
        ).start()

    def call_shards(u):
        def call(r, part):
            chip = chip_at(q, r)
            by = is_opposite(q, chip)
            holder = jnp.where(by, 4 * (q // 4) + lax.rem(chip, 4), chip)

            @pl.when(chip != q)
            def _():
                pl.semaphore_signal(
                    go.at[jnp.where(by, 2 + part, part)],
                    inc=1,
                    device_id=(2 * holder + core, z),
                    device_id_type=MESH,
                )

        j = u // 4 + GU_LEAD
        k = (u - GU_CHUNKS + DN_LEAD) // 2

        @pl.when(is_first & (lax.rem(u, 4) == 0) & (j < n))
        def _():
            call(j, 0)

        @pl.when(is_first & (lax.rem(u, 2) == 0) & (u >= GU_CHUNKS - DN_LEAD) & (k < n))
        def _():
            call(k, 1)

    def beside(u):
        call_shards(u)

        @pl.when(u == gu_call)
        def _():
            send_shard_on_call(0)

        @pl.when(u == dn_call)
        def _():
            send_shard_on_call(1)

        @pl.when(u == gu_other_call)
        def _():
            send_other_on_call(0)

        @pl.when(u == dn_other_call)
        def _():
            send_other_on_call(1)

        k = (u - row_call) // ROW_EVERY

        @pl.when((u >= row_call) & (lax.rem(u - row_call, ROW_EVERY) == 0))
        def _():
            @pl.when(k < n - 1)
            def _():
                send_rows(k + 1, send_t, in_t, row_send.at[0], row_recv.at[0])

            @pl.when((k >= n - 1) & (k < 2 * (n - 1)))
            def _():
                send_rows(k - n + 2, send_g, in_g, row_send.at[1], row_recv.at[1])

    def wait_group(g, sems):
        group = gu.at[pl.ds(0, 8 * GU_PIECE), :]
        pltpu.make_async_copy(group, group, sems.at[number(8 * g) // 8]).wait()

    def wait_step(g, carry):
        wait_group(g, sib)
        return carry

    tile = min(256, ff)

    def wait_gate_up():
        lax.fori_loop(2 * GU_CHUNKS // 8, CHUNKS // 8, wait_step, 0)
        arrived_rows(in_t, row_recv.at[0])

    def gate_up(j):
        cols = rows_of(j * tile, tile)
        gate[:, cols] = dot(in_t[...], gu[:, cols])
        up[:, cols] = dot(in_t[...], gu[:, rows_of(ff + j * tile, tile)])
        hidden[:, cols] = (jax.nn.silu(gate[:, cols]) * up[:, cols]).astype(jnp.bfloat16)

    other_late = jnp.where(upward, OTHER_UP - OTHER_STEP * dist, OTHER_DOWN - OTHER_STEP * dist)
    gate_up_at = GU_CHUNKS + jnp.maximum(other_late, 0) + MARGIN
    is_early = (gate_up_at + 2 * (ff // tile) < own) & jnp.logical_not(is_first)
    gate_up_at = jnp.where(is_early, gate_up_at, CHUNKS)

    def gu_step(u, carry):
        beside(u)
        take(gu_chunk(u), u)
        return carry

    def dn_step(u, carry):
        beside(u)
        take(dn_chunk(u), u)
        j = (u - gate_up_at) // 2

        @pl.when(u == gate_up_at)
        def _():
            wait_gate_up()

        @pl.when((u >= gate_up_at) & (lax.rem(u - gate_up_at, 2) == 0) & (j < ff // tile))
        def _():
            gate_up(j)

        return carry

    lax.fori_loop(0, GU_CHUNKS, gu_step, 0)
    lax.fori_loop(GU_CHUNKS, own, dn_step, 0)

    def group_step(g, carry):
        wait_group(g, sib)

        def one(k, carry):
            pass_on(dn_chunk(8 * g + k), 8 * g + k)
            return carry

        lax.fori_loop(0, 8, one, 0)
        return carry

    seen = jnp.maximum(own, passed) // 8
    lax.fori_loop(own // 8, seen, group_step, 0)

    @pl.when(jnp.logical_not(is_early))
    def _():
        wait_gate_up()

        def gate_up_step(j, carry):
            gate_up(j)
            return carry

        lax.fori_loop(0, ff // tile, gate_up_step, 0)

    lax.fori_loop(seen, 2 * GU_CHUNKS // 8, wait_step, 0)

    kept_width = width * capacity // SLOTS
    parts = kept_width // WIDE
    row = lax.broadcasted_iota(jnp.int32, (slots, slots), 0)
    col = lax.broadcasted_iota(jnp.int32, (slots, slots), 1)

    def folds(row, col, part):
        r = row // SLOTS * SLOTS + (lax.rem(row, SLOTS) - capacity) * parts + part
        return jnp.where((lax.rem(row, SLOTS) >= capacity) & (col == r), 1.0, 0.0).astype(jnp.bfloat16)

    fold = [folds(row, col, part) for part in range(parts)]

    def packed(value, place):
        last = value(parts).astype(jnp.bfloat16)
        for part in range(parts):
            place[:, part * WIDE : (part + 1) * WIDE] = (value(part) + dot(fold[part], last)).astype(jnp.bfloat16)

    packed(lambda j: dot_nt(hidden[...], dn[j * WIDE : (j + 1) * WIDE, :]), out_s)
    scatter_rows(out_s, back_o, back_send.at[0], back_recv.at[0])

    arrived_rows(in_g, row_recv.at[1])

    def grad_hidden_step(j, carry):
        cols = rows_of(j * tile, tile)
        grad_hidden = dot(in_g[...], dn[:, cols])
        g = gate[:, cols]
        s = jax.nn.sigmoid(g)
        ggu[:, cols] = (grad_hidden * up[:, cols] * s * (1.0 + g * (1.0 - s))).astype(jnp.bfloat16)
        ggu[:, rows_of(ff + j * tile, tile)] = (grad_hidden * g * s).astype(jnp.bfloat16)
        return carry

    lax.fori_loop(0, ff // tile, grad_hidden_step, 0)
    packed(lambda j: dot_nt(ggu[...], gu[j * WIDE : (j + 1) * WIDE, :]), eg_s)
    scatter_rows(eg_s, back_g, back_send.at[1], back_recv.at[1])

    by_token = jnp.transpose(weight_of)
    first = by_token.astype(jnp.bfloat16)
    rest = by_token - first.astype(jnp.float32)
    second = rest.astype(jnp.bfloat16)
    third = (rest - second.astype(jnp.float32)).astype(jnp.bfloat16)
    by_slot[...] = jnp.transpose(chosen).astype(jnp.bfloat16)
    arrived_rows(back_o, back_recv.at[0])
    unfold = [folds(col, row, part) for part in range(parts)]
    last = sum(dot(unfold[part], back_o[:, part * WIDE : (part + 1) * WIDE]) for part in range(parts))
    products = jnp.zeros((slots, tok_rows), jnp.float32)
    for part in range(parts + 1):
        cols = slice(part * WIDE, (part + 1) * WIDE)
        out = back_o[:, cols] if part < parts else last.astype(jnp.bfloat16)
        mixed[:, cols] = (dot(first, out) + (dot(second, out) + dot(third, out))).astype(jnp.bfloat16)
        products = products + dot_nt(out, cotangent[:, cols])
    products = jnp.where(kept, products, 0.0)
    for k in range(top):
        hit = routes[k : k + 1, :] == expert_of
        grad_gates[k : k + 1, :] = jnp.sum(jnp.where(hit, products, 0.0), axis=0, keepdims=True)

    def ring_sent(g, carry):
        wait_group(g, ring_send)
        return carry

    def sib_sent(g, carry):
        wait_group(g, sib_send)
        return carry

    lax.fori_loop(0, passed // 8, ring_sent, 0)
    lax.fori_loop(0, own // 8, sib_sent, 0)

    @pl.when(jnp.logical_not(is_target))
    def _():
        for part in range(2):
            pltpu.make_async_copy(others[part], others[part], shard_send.at[part]).wait()

    @pl.when(is_between)
    def _():
        for part in range(2):
            pltpu.make_async_copy(others[part], others[part], shard_send.at[2 + part]).wait()

    sent_rows(send_t, row_send.at[0])
    sent_rows(send_g, row_send.at[1])
    sent_rows(out_s, back_send.at[0])
    sent_rows(eg_s, back_send.at[1])
    arrived_rows(back_g, back_recv.at[1])


def finish(capacity, mixed, back, by_slot, mixed_out, grad_out, grad, sems):
    slots, kept_width = back.shape
    parts = kept_width // WIDE
    copy_mixed = pltpu.make_async_copy(mixed, mixed_out, sems.at[0])
    copy_mixed.start()
    row = lax.broadcasted_iota(jnp.int32, (slots, slots), 0)
    col = lax.broadcasted_iota(jnp.int32, (slots, slots), 1)
    block = col // SLOTS * SLOTS
    copies = [copy_mixed]
    last = jnp.zeros((slots, WIDE), jnp.float32)
    for part in range(parts + 1):
        cols = slice(part * WIDE, (part + 1) * WIDE)
        if part < parts:
            rows = back[:, cols]
            source = block + (lax.rem(col, SLOTS) - capacity) * parts + part
            unfold = jnp.where((lax.rem(col, SLOTS) >= capacity) & (row == source), 1.0, 0.0)
            last = last + dot(unfold.astype(jnp.bfloat16), rows)
        else:
            rows = last.astype(jnp.bfloat16)
        grad[:, cols] = dot(by_slot[...], rows).astype(jnp.bfloat16)
        copy = pltpu.make_async_copy(grad.at[:, cols], grad_out.at[:, cols], sems.at[part + 1])
        copy.start()
        copies.append(copy)
    for copy in copies:
        copy.wait()


def on_device(tokens, cotangent, routes, route_weights, gate_up_weight, down_weight):
    n = lax.axis_size("expert")
    tok_rows, width = tokens.shape
    top = routes.shape[1]
    shard, ff = down_weight.shape[1:]
    capacity = 3 * tok_rows // 32
    slots = n * SLOTS
    rows = pltpu.VMEM((slots, width), jnp.bfloat16)
    dma = pltpu.SemaphoreType.DMA
    hbm = pl.BlockSpec(memory_space=pltpu.HBM)
    vmem = pl.BlockSpec(memory_space=pltpu.VMEM)
    kept_width = width * capacity // SLOTS
    packed_rows = pltpu.VMEM((slots, kept_width), jnp.bfloat16)
    mixed, back, by_slot, grad_gates = pl.pallas_call(
        functools.partial(kernel, n, capacity),
        out_shape=(
            jax.ShapeDtypeStruct((tok_rows, width), jnp.bfloat16),
            jax.ShapeDtypeStruct((slots, kept_width), jnp.bfloat16),
            jax.ShapeDtypeStruct((tok_rows, slots), jnp.bfloat16),
            jax.ShapeDtypeStruct((top, tok_rows), jnp.float32),
        ),
        in_specs=[hbm, hbm, vmem, vmem, hbm, hbm],
        out_specs=[vmem] * 4,
        scratch_shapes=[
            pltpu.VMEM((tok_rows, width), jnp.bfloat16),
            pltpu.VMEM((tok_rows, width), jnp.bfloat16),
            pltpu.VMEM((width, 2 * ff), jnp.bfloat16),
            pltpu.VMEM((width, ff), jnp.bfloat16),
            rows,
            rows,
            rows,
            rows,
            pltpu.VMEM((slots, ff), jnp.float32),
            pltpu.VMEM((slots, ff), jnp.float32),
            pltpu.VMEM((slots, ff), jnp.bfloat16),
            pltpu.VMEM((slots, 2 * ff), jnp.bfloat16),
            packed_rows,
            packed_rows,
            packed_rows,
            pltpu.VMEM((shard, 2 * ff), jnp.bfloat16),
            pltpu.VMEM((shard, ff), jnp.bfloat16),
            dma((2,)),
            dma((CHUNKS,)),
            dma((CHUNKS // 8,)),
            dma((CHUNKS // 8,)),
            dma((CHUNKS // 8,)),
            dma((4,)),
            dma((2,)),
            dma((2,)),
            dma((2,)),
            dma((2,)),
            dma((2,)),
            pltpu.SemaphoreType.REGULAR((4,)),
        ],
        compiler_params=pltpu.CompilerParams(
            collective_id=0, has_side_effects=True, vmem_limit_bytes=28 * 1024 * 1024
        ),
    )(tokens, cotangent, routes.T, route_weights.T, gate_up_weight, down_weight)
    mixed, grad_tokens = pl.pallas_call(
        functools.partial(finish, capacity),
        out_shape=(
            jax.ShapeDtypeStruct((tok_rows, width), jnp.bfloat16),
            jax.ShapeDtypeStruct((tok_rows, width), jnp.bfloat16),
        ),
        in_specs=[vmem] * 3,
        out_specs=[hbm] * 2,
        scratch_shapes=[
            pltpu.VMEM((tok_rows, width), jnp.bfloat16),
            dma((2 + kept_width // WIDE,)),
        ],
        compiler_params=pltpu.CompilerParams(vmem_limit_bytes=16 * 1024 * 1024),
    )(mixed, back, by_slot)
    return mixed, grad_tokens, grad_gates.T


def solution(mesh):
    rows = P(("fsdp", "expert"), None)
    weight = P("expert", "fsdp", None)
    return jax.shard_map(
        on_device,
        mesh=mesh,
        in_specs=(rows, rows, rows, rows, weight, weight),
        out_specs=(rows, rows, rows),
        check_vma=False,
    )
```

time: 166 us -> 138 us (0.83)
  Pallas kernels: 161 us -> 129 us
  local copies, waits for them, and re-layouts: 3.33 us -> 5.86 us
    pallas_call x1, Pallas kernels: 161 us -> 128 us  [on_device(): pl.pallas_call(functools.partial(kernel, n, capacity), out_shape=(jax.Sha...]
    unnamed x7 -> x13, local copies, waits for them, and re-layouts: 3.33 us -> 5.86 us
where the time goes in v3:
time: 138 us; the launch traced here: 136 us
  Pallas kernels  129 us (93%)
  local copies, waits for them, and re-layouts  5.86 us (4%)
    pallas_call x1, Pallas kernels, on_device(): pl.pallas_call(functools.partial(kernel, n, capacity), out_shape=(jax.Sha...  128 us
    unnamed x13, local copies, waits for them, and re-layouts  5.86 us

profile of v3, /device:TPU:1, one launch (start us, length us, event | category | flops | bytes accessed | tf_op | source)
XLA Modules:
  0.0 135.6 jit_solution(4642060361725685657)
XLA Ops:
  0.6 0.0 copy-start
  0.6 1.0 copy-done
  1.7 0.0 copy-start.1
  1.7 1.0 copy-done.1
  2.7 0.0 copy-start.2
  2.7 0.9 copy-done.2
  3.6 0.0 copy-start.3
  3.6 0.9 copy-done.3
  4.5 0.0 copy-start.4
  4.5 0.7 copy-done.4
  5.2 0.0 copy-start.5
  5.2 0.7 copy-done.5
  5.9 127.8 %shard_map.85 = (bf16[128,2048]{1,0:T(8,128)(2,1)S(1)}, bf16[256,1536]{1,0:T(8,128)(2,1)S(1)}, bf16[128,256]{1,0:T(8,128)(2,1)S(1)}, f32[8,128]{1,0:T(8,128)S(1)}) custom-call(bf16[128,2048]{1,0:T(8,128)(2,1)S(1)} %copy-done, bf16[128,2048]{1,0:T(8,128)(2,1)S(1)} %copy-done.1, s32[8,128]{1,0:T(8,128)S(1)} %bitcast.3, f32[8,128]{1,0:T(8,128)S(1)} %bitcast.4, ...), custom_call_target="tpu_custom_call" | custom-call | tf_op jit(solution)/shard_map/pallas_call | solution.py:593
  133.7 1.3 shard_map.86
  135.0 0.6 copy.10
Async XLA Ops:
  0.6 1.0 copy-start
  1.7 1.0 copy-start.1
  2.7 0.9 copy-start.2
  3.6 0.9 copy-start.3
  4.5 0.7 copy-start.4
  5.2 0.7 copy-start.5

commit v4 on v3

--- a/solution.py
+++ b/solution.py
@@ -14,12 +14,16 @@
 GU_CHUNKS = 64
 CHUNKS = 3 * GU_CHUNKS
 MEET_FIRST, MEET_STEP = 130, 5
-GU_LEAD, DN_LEAD = 5, 20
+AT_ONCE, GU_LEAD, DN_LEAD = 7, 7, 20
 HOP, SLACK = 6, 8
 ROW_CALL, ROW_EVERY = 110, 2
 OTHER_UP, OTHER_DOWN, OTHER_STEP = 77, 98, 11
 MARGIN = 10
 WIDE = 512
+FAR_FIRST = sorted(
+    ((k % 4, k // 4) for k in range(1, 16)),
+    key=lambda step: -sum(min(a, 4 - a) for a in step),
+)
 NT = (((1,), (1,)), ((), ()))
 
 
@@ -43,8 +47,13 @@
 
 
 def chip_at(q, r):
-    k = r // 2
-    h = jnp.where(lax.rem(r, 2) == 0, q // 8, 1 - q // 8)
+    m = r // 3
+    turn = r - 3 * m
+    beyond = (turn == 2) | ((turn == 0) & (m >= 3))
+    k_beyond = jnp.where(turn == 2, m, m + 2)
+    k_near = jnp.where(turn == 1, jnp.where(m == 0, 1, m + 3), m + jnp.where(m > 0, 1, 0))
+    k = jnp.where(beyond, k_beyond, k_near)
+    h = jnp.where(beyond, 1 - q // 8, q // 8)
     near = nearest_row(q, h)
     row = jnp.where(k < 4, near, 4 * h + 1 - near)
     d = lax.rem(k, 4)
@@ -56,7 +65,10 @@
     near = nearest_row(q, c // 8)
     off = lax.rem(lax.rem(c, 4) - lax.rem(q, 4) + 4, 4)
     d = off - jnp.where(off == 3, 1, 0) + jnp.where(off == 2, 1, 0)
-    return 2 * (jnp.where(c // 4 == near, 0, 4) + d) + jnp.where(c // 8 == q // 8, 0, 1)
+    k = jnp.where(c // 4 == near, 0, 4) + d
+    of_near = jnp.where(k < 2, k, jnp.where(k < 4, 3 * k - 3, 3 * k - 8))
+    of_beyond = jnp.where(k < 5, 3 * k + 2, 3 * k - 6)
+    return jnp.where(c // 8 == q // 8, of_near, of_beyond)
 
 
 def is_opposite(q, c):
@@ -130,14 +142,103 @@
     barrier = pltpu.get_barrier_semaphore()
 
     def greet(k, carry):
-        pl.semaphore_signal(
-            barrier, inc=1, device_id=(lax.rem(me + k, 2 * n), z), device_id_type=MESH
-        )
+        other = 2 * lax.rem(q + k, n) + core
+        pl.semaphore_signal(barrier, inc=1, device_id=(other, z), device_id_type=MESH)
         return carry
 
     pl.semaphore_signal(barrier, inc=1, device_id=(me, after), device_id_type=MESH)
     pl.semaphore_signal(barrier, inc=1, device_id=(me, before), device_id_type=MESH)
-    lax.fori_loop(1, 2 * n, greet, 0)
+    pl.semaphore_signal(barrier, inc=1, device_id=(sibling, z), device_id_type=MESH)
+    lax.fori_loop(1, n, greet, 0)
+
+    pl.semaphore_wait(barrier, n + 2)
+
+    def meet(d):
+        return jnp.minimum(jnp.maximum(8 * ((MEET_FIRST - MEET_STEP * d + 4) // 8), GU_CHUNKS), 2 * GU_CHUNKS)
+
+    d = lax.rem(z - q + n, n)
+    dist = jnp.where(upward, d, lax.rem(n - d, n))
+    next_d = jnp.where(upward, d + 1, lax.rem(d + n - 1, n))
+    is_first = d == 0
+    own = jnp.where(is_first, CHUNKS // 2, jnp.where(upward, meet(d), CHUNKS - meet(d)))
+    passed = jnp.where(upward, meet(next_d), CHUNKS - meet(next_d))
+    passed = jnp.where((next_d == 0) | (next_d == n), 0, passed)
+
+    def number(u):
+        return jnp.where(upward, u, CHUNKS - 1 - u)
+
+    is_target = q == z
+    opposite = lax.rem(q + n // 2, n)
+    goes_by = is_opposite(z, q)
+    is_between = is_opposite(z, opposite)
+    between = 4 * (z // 4) + lax.rem(q, 4)
+
+    def place_in_order(t):
+        return jnp.where(upward, t, CHUNKS - 1 - t)
+
+    def shard_chunks(part, source, chip):
+        owner, rank = 2 * chip + core, rank_of(z, chip)
+        size, weight, at = ((GU_PIECE, gu, 4 * rank), (DN_PIECE, dn, GU_CHUNKS + 2 * rank))[part]
+        for p in range(shard // size):
+            yield (
+                source.at[pl.ds(p * size, size), :],
+                weight.at[rows_of(owner * shard + p * size, size), :],
+                ring.at[place_in_order(at + p)],
+            )
+
+    shards = (gu_shard.at[0], dn_shard.at[0])
+    others = (gu_other, dn_other)
+
+    def send_shard(part):
+        for source, place, sem in shard_chunks(part, shards[part], q):
+            pltpu.make_async_remote_copy(
+                source, place, shard_send.at[part], sem, device_id=(2 * z + core, z), device_id_type=MESH
+            ).start()
+
+    def send_shard_on_call(part):
+        pl.semaphore_wait(go.at[part], 1)
+        send_shard(part)
+
+    def send_other_on_call(part):
+        pltpu.make_async_copy(others[part], others[part], other_recv.at[part]).wait()
+        pl.semaphore_wait(go.at[2 + part], 1)
+        for source, place, sem in shard_chunks(part, others[part], opposite):
+            pltpu.make_async_remote_copy(
+                source, place, shard_send.at[2 + part], sem, device_id=(2 * z + core, z), device_id_type=MESH
+            ).start()
+
+    def calls(rank):
+        gu_call = 4 * (rank - GU_LEAD) - HOP * dist + SLACK
+        dn_call = GU_CHUNKS + 2 * rank - DN_LEAD - HOP * dist + SLACK
+        return gu_call, dn_call
+
+    rank = rank_of(z, q)
+    at_once = rank < AT_ONCE
+    is_direct = jnp.logical_not(is_target | goes_by)
+    gu_call, dn_call = calls(rank)
+    gu_other_call, dn_other_call = calls(rank_of(z, opposite))
+
+    @pl.when(is_target)
+    def _():
+        for part in range(2):
+            for source, place, sem in shard_chunks(part, shards[part], q):
+                pltpu.make_async_copy(source, place, sem).start()
+
+    @pl.when(goes_by)
+    def _():
+        for part in range(2):
+            pltpu.make_async_remote_copy(
+                shards[part],
+                others[part],
+                shard_send.at[part],
+                other_recv.at[part],
+                device_id=(2 * between + core, z),
+                device_id_type=MESH,
+            ).start()
+
+    @pl.when(is_direct & at_once)
+    def _():
+        send_shard(0)
 
     slot_id = lax.broadcasted_iota(jnp.int32, (slots, tok_rows), 0)
     expert_of = slot_id // SLOTS
@@ -162,95 +263,6 @@
     loads[1].wait()
     send_g[...] = (slot_weight * dot(picks, cotangent[...])).astype(jnp.bfloat16)
 
-    pl.semaphore_wait(barrier, 2 * n + 1)
-
-    def meet(d):
-        return jnp.minimum(jnp.maximum(8 * ((MEET_FIRST - MEET_STEP * d + 4) // 8), GU_CHUNKS), 2 * GU_CHUNKS)
-
-    d = lax.rem(z - q + n, n)
-    dist = jnp.where(upward, d, lax.rem(n - d, n))
-    next_d = jnp.where(upward, d + 1, lax.rem(d + n - 1, n))
-    is_first = d == 0
-    own = jnp.where(is_first, CHUNKS // 2, jnp.where(upward, meet(d), CHUNKS - meet(d)))
-    passed = jnp.where(upward, meet(next_d), CHUNKS - meet(next_d))
-    passed = jnp.where((next_d == 0) | (next_d == n), 0, passed)
-
-    def number(u):
-        return jnp.where(upward, u, CHUNKS - 1 - u)
-
-    is_target = q == z
-    opposite = lax.rem(q + n // 2, n)
-    goes_by = is_opposite(z, q)
-    is_between = is_opposite(z, opposite)
-    between = 4 * (z // 4) + lax.rem(q, 4)
-
-    def place_in_order(t):
-        return jnp.where(upward, t, CHUNKS - 1 - t)
-
-    def shard_chunks(part, source, chip):
-        owner, rank = 2 * chip + core, rank_of(z, chip)
-        size, weight, at = ((GU_PIECE, gu, 4 * rank), (DN_PIECE, dn, GU_CHUNKS + 2 * rank))[part]
-        for p in range(shard // size):
-            yield (
-                source.at[pl.ds(p * size, size), :],
-                weight.at[rows_of(owner * shard + p * size, size), :],
-                ring.at[place_in_order(at + p)],
-            )
-
-    shards = (gu_shard.at[0], dn_shard.at[0])
-    others = (gu_other, dn_other)
-
-    def send_shard(part):
-        for source, place, sem in shard_chunks(part, shards[part], q):
-            pltpu.make_async_remote_copy(
-                source, place, shard_send.at[part], sem, device_id=(2 * z + core, z), device_id_type=MESH
-            ).start()
-
-    def send_shard_on_call(part):
-        pl.semaphore_wait(go.at[part], 1)
-        send_shard(part)
-
-    def send_other_on_call(part):
-        pltpu.make_async_copy(others[part], others[part], other_recv.at[part]).wait()
-        pl.semaphore_wait(go.at[2 + part], 1)
-        for source, place, sem in shard_chunks(part, others[part], opposite):
-            pltpu.make_async_remote_copy(
-                source, place, shard_send.at[2 + part], sem, device_id=(2 * z + core, z), device_id_type=MESH
-            ).start()
-
-    def calls(rank):
-        gu_call = 4 * (rank - GU_LEAD) - HOP * dist + SLACK
-        dn_call = GU_CHUNKS + 2 * rank - DN_LEAD - HOP * dist + SLACK
-        return gu_call, dn_call
-
-    rank = rank_of(z, q)
-    at_once = rank < GU_LEAD
-    is_direct = jnp.logical_not(is_target | goes_by)
-    gu_call, dn_call = calls(rank)
-    gu_other_call, dn_other_call = calls(rank_of(z, opposite))
-
-    @pl.when(is_target)
-    def _():
-        for part in range(2):
-            for source, place, sem in shard_chunks(part, shards[part], q):
-                pltpu.make_async_copy(source, place, sem).start()
-
-    @pl.when(goes_by)
-    def _():
-        for part in range(2):
-            pltpu.make_async_remote_copy(
-                shards[part],
-                others[part],
-                shard_send.at[part],
-                other_recv.at[part],
-                device_id=(2 * between + core, z),
-                device_id_type=MESH,
-            ).start()
-
-    @pl.when(is_direct & at_once)
-    def _():
-        send_shard(0)
-
     @pl.when(is_direct & jnp.logical_not(at_once) & (gu_call < 0))
     def _():
         send_shard_on_call(0)
@@ -288,13 +300,18 @@
             device_id_type=MESH,
         ).start()
 
-    def scatter_rows(source, place, send_sem, recv_sem):
-        def step(k, carry):
-            send_rows(k, source, place, send_sem, recv_sem)
-            return carry
-
+    def return_rows(source, place, send_sem, recv_sem):
         keep_rows(source, place, recv_sem)
-        lax.fori_loop(1, n, step, 0)
+        for dx, dy in FAR_FIRST:
+            other = 4 * lax.rem(q // 4 + dy, 4) + lax.rem(lax.rem(q, 4) + dx, 4)
+            pltpu.make_async_remote_copy(
+                source.at[rows_of(other * SLOTS, SLOTS), :],
+                place.at[mine, :],
+                send_sem,
+                recv_sem,
+                device_id=(2 * other + core, z),
+                device_id_type=MESH,
+            ).start()
 
     def sent_rows(source, send_sem):
         rest = source.at[pl.ds(0, (n - 1) * SLOTS), :]
@@ -356,6 +373,11 @@
         j = u // 4 + GU_LEAD
         k = (u - GU_CHUNKS + DN_LEAD) // 2
 
+        @pl.when(is_first & (u == 0))
+        def _():
+            for r in range(AT_ONCE, GU_LEAD):
+                call(r, 0)
+
         @pl.when(is_first & (lax.rem(u, 4) == 0) & (j < n))
         def _():
             call(j, 0)
@@ -485,7 +507,7 @@
             place[:, part * WIDE : (part + 1) * WIDE] = (value(part) + dot(fold[part], last)).astype(jnp.bfloat16)
 
     packed(lambda j: dot_nt(hidden[...], dn[j * WIDE : (j + 1) * WIDE, :]), out_s)
-    scatter_rows(out_s, back_o, back_send.at[0], back_recv.at[0])
+    return_rows(out_s, back_o, back_send.at[0], back_recv.at[0])
 
     arrived_rows(in_g, row_recv.at[1])
 
@@ -500,7 +522,7 @@
 
     lax.fori_loop(0, ff // tile, grad_hidden_step, 0)
     packed(lambda j: dot_nt(ggu[...], gu[j * WIDE : (j + 1) * WIDE, :]), eg_s)
-    scatter_rows(eg_s, back_g, back_send.at[1], back_recv.at[1])
+    return_rows(eg_s, back_g, back_send.at[1], back_recv.at[1])
 
     by_token = jnp.transpose(weight_of)
     first = by_token.astype(jnp.bfloat16)
@@ -550,19 +572,51 @@
     arrived_rows(back_g, back_recv.at[1])
 
 
-def finish(capacity, mixed, back, by_slot, mixed_out, grad_out, grad, sems):
+def finish(
+    capacity,
+    mixed_hbm,
+    back_hbm,
+    by_slot_hbm,
+    gates_hbm,
+    mixed_out,
+    grad_out,
+    gates_out,
+    mixed,
+    back,
+    by_slot,
+    gates,
+    grad,
+    sems,
+    out_sems,
+):
     slots, kept_width = back.shape
     parts = kept_width // WIDE
-    copy_mixed = pltpu.make_async_copy(mixed, mixed_out, sems.at[0])
-    copy_mixed.start()
+    get_slot = pltpu.make_async_copy(by_slot_hbm, by_slot, sems.at[parts])
+    get_slot.start()
+    gets = []
+    for part in range(parts):
+        cols = slice(part * WIDE, (part + 1) * WIDE)
+        gets.append(pltpu.make_async_copy(back_hbm.at[:, cols], back.at[:, cols], sems.at[part]))
+        gets[part].start()
+    passing = [
+        pltpu.make_async_copy(mixed_hbm, mixed, sems.at[parts + 1]),
+        pltpu.make_async_copy(gates_hbm, gates, sems.at[parts + 2]),
+    ]
+    for copy in passing:
+        copy.start()
     row = lax.broadcasted_iota(jnp.int32, (slots, slots), 0)
     col = lax.broadcasted_iota(jnp.int32, (slots, slots), 1)
     block = col // SLOTS * SLOTS
-    copies = [copy_mixed]
+    copies = [
+        pltpu.make_async_copy(mixed, mixed_out, out_sems.at[parts + 1]),
+        pltpu.make_async_copy(gates, gates_out, out_sems.at[parts + 2]),
+    ]
+    get_slot.wait()
     last = jnp.zeros((slots, WIDE), jnp.float32)
     for part in range(parts + 1):
         cols = slice(part * WIDE, (part + 1) * WIDE)
         if part < parts:
+            gets[part].wait()
             rows = back[:, cols]
             source = block + (lax.rem(col, SLOTS) - capacity) * parts + part
             unfold = jnp.where((lax.rem(col, SLOTS) >= capacity) & (row == source), 1.0, 0.0)
@@ -570,9 +624,12 @@
         else:
             rows = last.astype(jnp.bfloat16)
         grad[:, cols] = dot(by_slot[...], rows).astype(jnp.bfloat16)
-        copy = pltpu.make_async_copy(grad.at[:, cols], grad_out.at[:, cols], sems.at[part + 1])
+        copy = pltpu.make_async_copy(grad.at[:, cols], grad_out.at[:, cols], out_sems.at[part])
         copy.start()
         copies.append(copy)
+        if part < 2:
+            passing[part].wait()
+            copies[part].start()
     for copy in copies:
         copy.wait()
 
@@ -586,7 +643,7 @@
     slots = n * SLOTS
     rows = pltpu.VMEM((slots, width), jnp.bfloat16)
     dma = pltpu.SemaphoreType.DMA
-    hbm = pl.BlockSpec(memory_space=pltpu.HBM)
+    hbm = pl.BlockSpec(memory_space=pl.ANY)
     vmem = pl.BlockSpec(memory_space=pltpu.VMEM)
     kept_width = width * capacity // SLOTS
     packed_rows = pltpu.VMEM((slots, kept_width), jnp.bfloat16)
@@ -632,23 +689,29 @@
             pltpu.SemaphoreType.REGULAR((4,)),
         ],
         compiler_params=pltpu.CompilerParams(
-            collective_id=0, has_side_effects=True, vmem_limit_bytes=28 * 1024 * 1024
+            collective_id=0, has_side_effects=True, vmem_limit_bytes=56 * 1024 * 1024
         ),
     )(tokens, cotangent, routes.T, route_weights.T, gate_up_weight, down_weight)
-    mixed, grad_tokens = pl.pallas_call(
+    mixed, grad_tokens, grad_gates = pl.pallas_call(
         functools.partial(finish, capacity),
         out_shape=(
             jax.ShapeDtypeStruct((tok_rows, width), jnp.bfloat16),
             jax.ShapeDtypeStruct((tok_rows, width), jnp.bfloat16),
+            jax.ShapeDtypeStruct((top, tok_rows), jnp.float32),
         ),
-        in_specs=[vmem] * 3,
-        out_specs=[hbm] * 2,
+        in_specs=[hbm] * 4,
+        out_specs=[hbm] * 3,
         scratch_shapes=[
             pltpu.VMEM((tok_rows, width), jnp.bfloat16),
-            dma((2 + kept_width // WIDE,)),
+            pltpu.VMEM((slots, kept_width), jnp.bfloat16),
+            pltpu.VMEM((tok_rows, slots), jnp.bfloat16),
+            pltpu.VMEM((top, tok_rows), jnp.float32),
+            pltpu.VMEM((tok_rows, width), jnp.bfloat16),
+            dma((3 + kept_width // WIDE,)),
+            dma((3 + kept_width // WIDE,)),
         ],
-        compiler_params=pltpu.CompilerParams(vmem_limit_bytes=16 * 1024 * 1024),
-    )(mixed, back, by_slot)
+        compiler_params=pltpu.CompilerParams(vmem_limit_bytes=56 * 1024 * 1024),
+    )(mixed, back, by_slot, grad_gates)
     return mixed, grad_tokens, grad_gates.T
 
 

time: 138 us -> 131 us (0.949); the launches traced: 136 us -> 131 us
  local copies, waits for them, and re-layouts: 5.86 us -> 0 us
    unnamed x13 -> x0, local copies, waits for them, and re-layouts: 5.86 us -> none
    pallas_call x1, Pallas kernels: 1.31 us -> 2.82 us  [on_device(): pl.pallas_call(functools.partial(finish, capacity), out_shape=(jax.ShapeD...]
where the time goes in v4:
time: 131 us
  Pallas kernels  130 us (99%)
    pallas_call x1, Pallas kernels, on_device(): pl.pallas_call(functools.partial(kernel, n, capacity), out_shape=(jax.Sha...  127 us
    pallas_call x1, Pallas kernels, on_device(): pl.pallas_call(functools.partial(finish, capacity), out_shape=(jax.ShapeD...  2.82 us

profile of v4, /device:TPU:1, one launch (start us, length us, event | category | flops | bytes accessed | tf_op | source)
XLA Modules:
  0.0 130.7 jit_solution(10962728914093275516)
XLA Ops:
  0.6 127.2 %shard_map.85 = (bf16[128,2048]{1,0:T(8,128)(2,1)}, bf16[256,1536]{1,0:T(8,128)(2,1)}, bf16[128,256]{1,0:T(8,128)(2,1)}, f32[8,128]{1,0:T(8,128)}) custom-call(bf16[128,2048]{1,0:T(8,128)(2,1)} %tokens_hbm.1, bf16[128,2048]{1,0:T(8,128)(2,1)} %cotangent_hbm.1, s32[8,128]{1,0:T(8,128)} %bitcast.3, f32[8,128]{1,0:T(8,128)} %bitcast.4, ...), custom_call_target="tpu_custom_call" | custom-call | tf_op jit(solution)/shard_map/pallas_call | solution.py:650
  127.9 2.8 %shard_map.86 = (bf16[128,2048]{1,0:T(8,128)(2,1)}, bf16[128,2048]{1,0:T(8,128)(2,1)}, f32[8,128]{1,0:T(8,128)}) custom-call(bf16[128,2048]{1,0:T(8,128)(2,1)} %get-tuple-element.10.mixed_hbm, bf16[256,1536]{1,0:T(8,128)(2,1)} %get-tuple-element.11.back_hbm, bf16[128,256]{1,0:T(8,128)(2,1)} %get-tuple-element.12.by_slot_hbm, ...), custom_call_target="tpu_custom_call" | custom-call | tf_op jit(solution)/shard_map/pallas_call | solution.py:695

commit v5 on v4

--- a/solution.py
+++ b/solution.py
@@ -14,11 +14,12 @@
 GU_CHUNKS = 64
 CHUNKS = 3 * GU_CHUNKS
 MEET_FIRST, MEET_STEP = 130, 5
-AT_ONCE, GU_LEAD, DN_LEAD = 7, 7, 20
+AT_ONCE, GU_LEAD, DN_LEAD = 7, 8, 16
 HOP, SLACK = 6, 8
 ROW_CALL, ROW_EVERY = 110, 2
 OTHER_UP, OTHER_DOWN, OTHER_STEP = 77, 98, 11
 MARGIN = 10
+PREPARE_AT = 32
 WIDE = 512
 FAR_FIRST = sorted(
     ((k % 4, k // 4) for k in range(1, 16)),
@@ -105,6 +106,8 @@
     back_o,
     gu_other,
     dn_other,
+    weight_of,
+    chosen,
     load,
     ring,
     sib,
@@ -240,28 +243,34 @@
     def _():
         send_shard(0)
 
-    slot_id = lax.broadcasted_iota(jnp.int32, (slots, tok_rows), 0)
-    expert_of = slot_id // SLOTS
-    slot_of = slot_id - expert_of * SLOTS
-    weight_of = jnp.zeros((slots, tok_rows), jnp.float32)
-    named = jnp.zeros((slots, tok_rows), jnp.float32)
-    for k in range(top):
-        hit = routes[k : k + 1, :] == expert_of
-        named = jnp.where(hit, 1.0, named)
-        weight_of = jnp.where(hit, route_weights[k : k + 1, :], weight_of)
-    row_id = lax.broadcasted_iota(jnp.int32, (tok_rows, tok_rows), 0)
-    col_id = lax.broadcasted_iota(jnp.int32, (tok_rows, tok_rows), 1)
-    above = jnp.where(row_id < col_id, 1.0, 0.0).astype(jnp.bfloat16)
-    earlier = dot(named.astype(jnp.bfloat16), above).astype(jnp.int32)
-    kept = (named > 0.5) & (earlier == slot_of) & (slot_of < capacity)
-    chosen = jnp.where(kept, 1.0, 0.0)
-    weight_of = jnp.where(kept, weight_of, 0.0)
-    picks = chosen.astype(jnp.bfloat16)
-    slot_weight = jnp.sum(weight_of, axis=1, keepdims=True)
-    loads[0].wait()
-    send_t[...] = dot(picks, tokens[...]).astype(jnp.bfloat16)
-    loads[1].wait()
-    send_g[...] = (slot_weight * dot(picks, cotangent[...])).astype(jnp.bfloat16)
+    expert_of = lax.broadcasted_iota(jnp.int32, (slots, tok_rows), 0) // SLOTS
+
+    def prepare_rows():
+        slot_of = lax.broadcasted_iota(jnp.int32, (slots, tok_rows), 0) - expert_of * SLOTS
+        weight = jnp.zeros((slots, tok_rows), jnp.float32)
+        named = jnp.zeros((slots, tok_rows), jnp.float32)
+        for k in range(top):
+            hit = routes[k : k + 1, :] == expert_of
+            named = jnp.where(hit, 1.0, named)
+            weight = jnp.where(hit, route_weights[k : k + 1, :], weight)
+        row_id = lax.broadcasted_iota(jnp.int32, (tok_rows, tok_rows), 0)
+        col_id = lax.broadcasted_iota(jnp.int32, (tok_rows, tok_rows), 1)
+        above = jnp.where(row_id < col_id, 1.0, 0.0).astype(jnp.bfloat16)
+        earlier = dot(named.astype(jnp.bfloat16), above).astype(jnp.int32)
+        kept = (named > 0.5) & (earlier == slot_of) & (slot_of < capacity)
+        weight = jnp.where(kept, weight, 0.0)
+        weight_of[...] = weight
+        chosen[...] = jnp.where(kept, 1.0, 0.0)
+        picks = chosen[...].astype(jnp.bfloat16)
+        slot_weight = jnp.sum(weight, axis=1, keepdims=True)
+        loads[0].wait()
+        send_t[...] = dot(picks, tokens[...]).astype(jnp.bfloat16)
+        loads[1].wait()
+        send_g[...] = (slot_weight * dot(picks, cotangent[...])).astype(jnp.bfloat16)
+
+    @pl.when(jnp.logical_not(is_first))
+    def _():
+        prepare_rows()
 
     @pl.when(is_direct & jnp.logical_not(at_once) & (gu_call < 0))
     def _():
@@ -320,8 +329,6 @@
     def arrived_rows(place, recv_sem):
         pltpu.make_async_copy(place, place, recv_sem).wait()
 
-    keep_rows(send_t, in_t, row_recv.at[0])
-    keep_rows(send_g, in_g, row_recv.at[1])
     row_call = jnp.minimum(jnp.maximum(ROW_CALL - HOP * dist, 0), own - 2 * ROW_EVERY * (n - 1))
 
     def gu_chunk(u):
@@ -389,6 +396,10 @@
     def beside(u):
         call_shards(u)
 
+        @pl.when(is_first & (u == PREPARE_AT))
+        def _():
+            prepare_rows()
+
         @pl.when(u == gu_call)
         def _():
             send_shard_on_call(0)
@@ -409,6 +420,11 @@
 
         @pl.when((u >= row_call) & (lax.rem(u - row_call, ROW_EVERY) == 0))
         def _():
+            @pl.when(k == 0)
+            def _():
+                keep_rows(send_t, in_t, row_recv.at[0])
+                keep_rows(send_g, in_g, row_recv.at[1])
+
             @pl.when(k < n - 1)
             def _():
                 send_rows(k + 1, send_t, in_t, row_send.at[0], row_recv.at[0])
@@ -524,12 +540,12 @@
     packed(lambda j: dot_nt(ggu[...], gu[j * WIDE : (j + 1) * WIDE, :]), eg_s)
     return_rows(eg_s, back_g, back_send.at[1], back_recv.at[1])
 
-    by_token = jnp.transpose(weight_of)
+    by_token = jnp.transpose(weight_of[...])
     first = by_token.astype(jnp.bfloat16)
     rest = by_token - first.astype(jnp.float32)
     second = rest.astype(jnp.bfloat16)
     third = (rest - second.astype(jnp.float32)).astype(jnp.bfloat16)
-    by_slot[...] = jnp.transpose(chosen).astype(jnp.bfloat16)
+    by_slot[...] = jnp.transpose(chosen[...]).astype(jnp.bfloat16)
     arrived_rows(back_o, back_recv.at[0])
     unfold = [folds(col, row, part) for part in range(parts)]
     last = sum(dot(unfold[part], back_o[:, part * WIDE : (part + 1) * WIDE]) for part in range(parts))
@@ -539,7 +555,7 @@
         out = back_o[:, cols] if part < parts else last.astype(jnp.bfloat16)
         mixed[:, cols] = (dot(first, out) + (dot(second, out) + dot(third, out))).astype(jnp.bfloat16)
         products = products + dot_nt(out, cotangent[:, cols])
-    products = jnp.where(kept, products, 0.0)
+    products = products * chosen[...]
     for k in range(top):
         hit = routes[k : k + 1, :] == expert_of
         grad_gates[k : k + 1, :] = jnp.sum(jnp.where(hit, products, 0.0), axis=0, keepdims=True)
@@ -675,6 +691,8 @@
             packed_rows,
             pltpu.VMEM((shard, 2 * ff), jnp.bfloat16),
             pltpu.VMEM((shard, ff), jnp.bfloat16),
+            pltpu.VMEM((slots, tok_rows), jnp.float32),
+            pltpu.VMEM((slots, tok_rows), jnp.float32),
             dma((2,)),
             dma((CHUNKS,)),
             dma((CHUNKS // 8,)),

time: 131 us -> 130 us (level)
  no operation moved by 1% of the time
where the time goes in v5:
time: 130 us
  Pallas kernels  129 us (99%)
    pallas_call x1, Pallas kernels, on_device(): pl.pallas_call(functools.partial(kernel, n, capacity), out_shape=(jax.Sha...  127 us
    pallas_call x1, Pallas kernels, on_device(): pl.pallas_call(functools.partial(finish, capacity), out_shape=(jax.ShapeD...  2.82 us

profile of v5, /device:TPU:1, one launch (start us, length us, event | category | flops | bytes accessed | tf_op | source)
XLA Modules:
  0.0 130.0 jit_solution(5604018685995028085)
XLA Ops:
  0.6 126.6 %shard_map.85 = (bf16[128,2048]{1,0:T(8,128)(2,1)}, bf16[256,1536]{1,0:T(8,128)(2,1)}, bf16[128,256]{1,0:T(8,128)(2,1)}, f32[8,128]{1,0:T(8,128)}) custom-call(bf16[128,2048]{1,0:T(8,128)(2,1)} %tokens_hbm.1, bf16[128,2048]{1,0:T(8,128)(2,1)} %cotangent_hbm.1, s32[8,128]{1,0:T(8,128)} %bitcast.3, f32[8,128]{1,0:T(8,128)} %bitcast.4, ...), custom_call_target="tpu_custom_call" | custom-call | tf_op jit(solution)/shard_map/pallas_call | solution.py:666
  127.2 2.8 %shard_map.86 = (bf16[128,2048]{1,0:T(8,128)(2,1)}, bf16[128,2048]{1,0:T(8,128)(2,1)}, f32[8,128]{1,0:T(8,128)}) custom-call(bf16[128,2048]{1,0:T(8,128)(2,1)} %get-tuple-element.10.mixed_hbm, bf16[256,1536]{1,0:T(8,128)(2,1)} %get-tuple-element.11.back_hbm, bf16[128,256]{1,0:T(8,128)(2,1)} %get-tuple-element.12.by_slot_hbm, ...), custom_call_target="tpu_custom_call" | custom-call | tf_op jit(solution)/shard_map/pallas_call | solution.py:713
